TPU v7x, 256 devices: a whole 4x4x8 slice. The times are simulated.
256 devices in a mesh: blk: 4 (over z_lo), sample: 64 (over y, x, z_hi, core).
Axes of the slice: x: 4, y: 4, z: 8 (z_hi: 2, z_lo: 4; z = z_hi * 4 + z_lo), core: 2. Of those that a mesh axis runs over, the one named last changes fastest.
Arguments:
- labels: bfloat16 [64, 4096, 512], P('sample', 'blk'), may hold values from -6 to 6
- basis: bfloat16 [64, 4096, 1024], P('sample', 'blk'), may hold values from -0.01171875 to 0.01171875
- gains: float32 [1024], replicated, may hold values from 2 to 32
- tiles: bfloat16 [64, 16, 4, 256, 256], P('sample', 'blk'), may hold values from 0 to 0.0029296875
- tile_cols: int32 [64, 16, 4], P('sample', 'blk'), may hold values from 0 to 15
- tile_valid: int32 [64, 16, 4], P('sample', 'blk'), may hold values 0 or 1
Outputs:
- solution: float32 [64, 4096, 512], P('sample', 'blk')
- residual: float32 [64, 4096, 512], P('sample', 'blk')
All inputs are finite; a program needn't handle non-finite values. No bound on the sum of `tile_valid` on one device may be relied on, other than what follows from the above.
Results may differ from a plain program's by a relative error of at most 0.0022.
Values may be sent and summed in bfloat16 or wider, within the bound.
No kernel may reach another device: no remote copies, remote signals or barrier semaphores. Data moves between devices by JAX's collectives and lax.ppermute only.
A program may use at most 64 MiB of HBM per device.

v0:
```python
import functools

import jax
import jax.numpy as jnp
from jax import lax
from jax.experimental import pallas as pl
from jax.experimental.pallas import tpu as pltpu
from jax.sharding import Mesh, PartitionSpec as P

F32 = jnp.float32
BF16 = jnp.bfloat16
FINE = ("blk", "y", "x", "zh", "core")
SAMPLE = ("y", "x", "zh", "core")
PLANE = ("y", "x")
COLUMN = ("blk", "zh")
VMEM_SOME = 16 * 1024 * 1024
VMEM_ALL = 60 * 1024 * 1024
CHUNKS = 2


def params(limit=VMEM_SOME):
    return pltpu.CompilerParams(vmem_limit_bytes=limit)


def shift(value, axis, by):
    size = lax.axis_size(axis)
    return lax.ppermute(value, axis, [(i, (i + by) % size) for i in range(size)])


def along_line(value, by, skip):
    size = lax.axis_size("blk")
    if by > 0:
        pairs = [(i, i + 1) for i in range(skip, size - 1)]
    else:
        pairs = [(i, i - 1) for i in range(1, size - skip)]
    return lax.ppermute(value, "blk", pairs)


def both_ways(pair, skip):
    return along_line(pair[0], 1, skip), along_line(pair[1], -1, skip)


def all_sum(value, axis):
    total = value
    for part in [shift(value, axis, k) for k in range(1, lax.axis_size(axis))]:
        total = total + part
    return total


def to_all(value, axes):
    copies = jnp.broadcast_to(value[None], (lax.axis_size(axes),) + value.shape)
    return lax.all_to_all(copies, axes, 0, 0)


def project_kernel(place, basis, labels, out):
    @pl.when(pl.program_id(0) == 0)
    def _():
        out[...] = jnp.zeros_like(out)

    out[...] += lax.dot_general(
        basis[...], labels[...], (((0,), (0,)), ((), ())), preferred_element_type=F32
    )


def project(place, basis, labels, own):
    rows, classes = labels.shape
    half = basis.shape[1] // 2
    steps = 4
    part = rows // steps
    side = (lambda i, p: (i, p[0])) if own else (lambda i, p: (i, 1 - p[0]))
    return pl.pallas_call(
        project_kernel,
        grid_spec=pltpu.PrefetchScalarGridSpec(
            num_scalar_prefetch=1,
            grid=(steps,),
            in_specs=[
                pl.BlockSpec((part, half), side),
                pl.BlockSpec((part, classes), lambda i, p: (i, 0)),
            ],
            out_specs=pl.BlockSpec((half, classes), lambda i, p: (0, 0)),
        ),
        out_shape=jax.ShapeDtypeStruct((half, classes), F32),
        compiler_params=params(),
        cost_estimate=pl.CostEstimate(
            flops=2 * rows * half * classes, bytes_accessed=4 * rows * half, transcendentals=0
        ),
        name="project_own" if own else "project_other",
    )(place, basis, labels)


def degree_parts_kernel(cols, valid, tiles, rows_out, cols_out):
    step = pl.program_id(0)
    slots = tiles.shape[0]

    @pl.when(step == 0)
    def _():
        cols_out[...] = jnp.zeros_like(cols_out)

    total = jnp.zeros(tiles.shape[1:], F32)
    for t in range(slots):
        at = step * slots + t
        tile = tiles[t].astype(F32) * valid[at].astype(F32)
        total = total + tile
        cols_out[pl.ds(cols[at], 1), :] += jnp.sum(tile, axis=0, keepdims=True)
    rows_out[...] = jnp.sum(total, axis=1, keepdims=True)


def degree_parts(tiles, cols, valid, col_blocks, slots):
    count, size, _ = tiles.shape
    steps = count // slots
    return pl.pallas_call(
        degree_parts_kernel,
        grid_spec=pltpu.PrefetchScalarGridSpec(
            num_scalar_prefetch=2,
            grid=(steps,),
            in_specs=[pl.BlockSpec((slots, size, size), lambda i, c, v: (i, 0, 0))],
            out_specs=[
                pl.BlockSpec((size, 1), lambda i, c, v: (i, 0)),
                pl.BlockSpec((col_blocks, size), lambda i, c, v: (0, 0)),
            ],
        ),
        out_shape=[
            jax.ShapeDtypeStruct((steps * size, 1), F32),
            jax.ShapeDtypeStruct((col_blocks, size), F32),
        ],
        cost_estimate=pl.CostEstimate(
            flops=4 * tiles.size, bytes_accessed=2 * tiles.size, transcendentals=0
        ),
        name="degree_parts",
    )(cols, valid, tiles)


def spread_of(basis_own, basis_other, mine, theirs):
    return jnp.dot(basis_own[...], mine[...], preferred_element_type=F32) + jnp.dot(
        basis_other[...], theirs[...], preferred_element_type=F32
    )


def moves(sources, targets, sems, size, count):
    return [
        pltpu.make_async_copy(
            sources.at[pl.ds(k * size, size), :], targets.at[pl.ds(k * size, size), :], sems.at[k]
        )
        for k in range(count)
    ]


def start_at(copies, step):
    for k, copy in enumerate(copies):
        pl.when(step == k)(copy.start)


def wait_at(copies, step):
    for k, copy in enumerate(copies):
        pl.when(step == k)(copy.wait)


def spread_kernel(
    place, labels, own, other, mine, theirs, search, rounded, dots, v_search, sems
):
    step, steps = pl.program_id(0), pl.num_programs(0)
    size = labels.shape[0]

    @pl.when(step == 0)
    def _():
        dots[...] = jnp.zeros_like(dots)

    residual = labels[...].astype(F32)
    value = residual + spread_of(own, other, mine, theirs)
    rounded[...] = value.astype(BF16)
    v_search[pl.ds(pl.multiple_of(step * size, size), size), :] = value
    dots[...] += jnp.sum(residual * value, axis=0, keepdims=True)
    stores = moves(v_search, search, sems, size, v_search.shape[0] // size)
    start_at(stores, step)

    @pl.when(step == steps - 1)
    def _():
        for copy in stores:
            copy.wait()


def spread(place, labels, basis, mine, theirs, part, chunk):
    rows, classes = labels.shape
    half = mine.shape[0]
    width = classes // CHUNKS
    block = pl.BlockSpec((part, width), lambda i, p: (i, 0))
    columns = pl.BlockSpec((half, width), lambda i, p: (0, chunk))
    return pl.pallas_call(
        spread_kernel,
        grid_spec=pltpu.PrefetchScalarGridSpec(
            num_scalar_prefetch=1,
            grid=(rows // part,),
            in_specs=[
                pl.BlockSpec((part, width), lambda i, p: (i, chunk)),
                pl.BlockSpec((part, half), lambda i, p: (i, p[0])),
                pl.BlockSpec((part, half), lambda i, p: (i, 1 - p[0])),
                columns,
                columns,
            ],
            out_specs=[
                pl.BlockSpec(memory_space=pltpu.HBM),
                block,
                pl.BlockSpec((1, width), lambda i, p: (0, 0)),
            ],
            scratch_shapes=[
                pltpu.VMEM((rows, width), F32),
                pltpu.SemaphoreType.DMA((rows // part,)),
            ],
        ),
        out_shape=[
            jax.ShapeDtypeStruct((rows, width), F32),
            jax.ShapeDtypeStruct((rows, width), BF16),
            jax.ShapeDtypeStruct((1, width), F32),
        ],
        compiler_params=params(),
        cost_estimate=pl.CostEstimate(
            flops=4 * rows * half * width, bytes_accessed=16 * rows * width, transcendentals=0
        ),
        name=f"spread_{chunk}",
    )(place, labels, basis, basis, mine, theirs)


def apply_kernel(places, cols, valid, place, tiles, degree, search, own, *rest):
    pieces, (image, dots, panel, v_search, v_image, sems, in_sems, out_sems) = rest[:-8], rest[-8:]
    step, steps = pl.program_id(0), pl.num_programs(0)
    slots, size, _ = tiles.shape
    rows = own.shape[0]
    me = place[1]
    last = panel.shape[0] // rows - 1

    def copies(act):
        for k, (offset, start) in enumerate(places):
            owner = me + offset

            @pl.when(jnp.logical_and(owner >= 0, owner <= last))
            def _(k=k, owner=owner, start=start):
                at = pl.multiple_of(owner * rows + start, size)
                target = panel.at[pl.ds(at, pieces[k].shape[0]), :]
                act(pltpu.make_async_copy(pieces[k], target, sems.at[k]))

    blocks = v_search.shape[0] // size
    loads = moves(search, v_search, in_sems, size, blocks)
    stores = moves(v_image, image, out_sems, size, blocks)

    @pl.when(step == 0)
    def _():
        copies(lambda copy: copy.start())
        for copy in loads:
            copy.start()
        dots[...] = jnp.zeros_like(dots)
        panel[pl.ds(pl.multiple_of(me * rows, size), rows), :] = own[...]
        copies(lambda copy: copy.wait())

    wait_at(loads, step)
    here = pl.ds(pl.multiple_of(step * size, size), size)
    value = v_search[here, :]
    total = value + 0.5 * (degree[...] * value)
    for t in range(slots):
        at = step * slots + t
        block = panel[pl.ds(pl.multiple_of(cols[at] * size, size), size), :]
        product = jnp.dot(tiles[t], block, preferred_element_type=F32)
        total = total - (0.5 * valid[at].astype(F32)) * product
    v_image[here, :] = total
    dots[...] += jnp.sum(value * total, axis=0, keepdims=True)
    start_at(stores, step)

    @pl.when(step == steps - 1)
    def _():
        for copy in stores:
            copy.wait()


def apply(cols, valid, place, tiles, degree, search, own, placed, slots, chunk):
    rows, classes = search.shape
    count, size, _ = tiles.shape
    in_hbm = pl.BlockSpec(memory_space=pltpu.HBM)
    places = tuple(item[:2] for item in placed)
    pieces = [item[2] for item in placed]
    return pl.pallas_call(
        functools.partial(apply_kernel, places),
        grid_spec=pltpu.PrefetchScalarGridSpec(
            num_scalar_prefetch=3,
            grid=(count // slots,),
            in_specs=[
                pl.BlockSpec((slots, size, size), lambda i, c, v, p: (i, 0, 0)),
                pl.BlockSpec((size, 1), lambda i, c, v, p: (i, 0)),
                in_hbm,
                pl.BlockSpec((rows, classes), lambda i, c, v, p: (0, 0)),
            ]
            + [pl.BlockSpec(memory_space=pl.ANY)] * len(pieces),
            out_specs=[in_hbm, pl.BlockSpec((1, classes), lambda i, c, v, p: (0, 0))],
            scratch_shapes=[
                pltpu.VMEM((lax.axis_size("blk") * rows, classes), BF16),
                pltpu.VMEM((rows, classes), F32),
                pltpu.VMEM((rows, classes), F32),
                pltpu.SemaphoreType.DMA((len(pieces),)),
                pltpu.SemaphoreType.DMA((count // slots,)),
                pltpu.SemaphoreType.DMA((count // slots,)),
            ],
        ),
        out_shape=[
            jax.ShapeDtypeStruct((rows, classes), F32),
            jax.ShapeDtypeStruct((1, classes), F32),
        ],
        compiler_params=params(),
        cost_estimate=pl.CostEstimate(
            flops=2 * count * size * size * classes,
            bytes_accessed=20 * rows * classes,
            transcendentals=0,
        ),
        name=f"apply_{chunk}",
    )(cols, valid, place, tiles, degree, search, own, *pieces)


def step_kernel(sums, labels, *refs):
    searches, images = refs[:CHUNKS], refs[CHUNKS : 2 * CHUNKS]
    solution_out, residual_out = refs[2 * CHUNKS :]
    total = jnp.sum(sums[...], axis=0)
    size = total[0:1, :] / total[1:2, :]
    width = searches[0].shape[1]
    for k in range(CHUNKS):
        at = slice(k * width, (k + 1) * width)
        solution_out[:, at] = size[:, at] * searches[k][...]
        residual_out[:, at] = labels[:, at].astype(F32) - size[:, at] * images[k][...]


def take_step(sums, labels, searches, images, part):
    rows, classes = labels.shape
    block = pl.BlockSpec((part, classes), lambda i: (i, 0))
    piece = pl.BlockSpec((part, classes // CHUNKS), lambda i: (i, 0))
    return pl.pallas_call(
        step_kernel,
        grid=(rows // part,),
        in_specs=[pl.BlockSpec(sums.shape, lambda i: (0, 0, 0)), block] + [piece] * 2 * CHUNKS,
        out_specs=[block, block],
        out_shape=[jax.ShapeDtypeStruct((rows, classes), F32)] * 2,
        compiler_params=params(VMEM_ALL),
        name="take_step",
    )(sums, labels, *searches, *images)


def on_device(labels, basis, gains, tiles, tile_cols, tile_valid):
    labels, basis, tiles = labels[0], basis[0], tiles[0]
    rows_dev, classes = labels.shape
    row_blocks, slots, tile_size = tiles.shape[:3]
    group = lax.axis_size("blk")
    tiles = tiles.reshape(row_blocks * slots, tile_size, tile_size)
    blk, y, x, core = (lax.axis_index(a) for a in ("blk", "y", "x", "core"))
    place = jnp.stack([core, blk]).astype(jnp.int32)

    cols = tile_cols.reshape(-1)
    valid = tile_valid.reshape(-1)

    sent = shift(project(place, basis, labels, False), "core", 1)
    chip_sum = project(place, basis, labels, True) + sent
    chip_sum, later_tiles = lax.optimization_barrier((chip_sum, tiles))
    row_total, col_parts = degree_parts(later_tiles, cols, valid, row_blocks * group, slots)
    extra = rows_dev // classes
    col_parts = col_parts.reshape(group * extra, classes)
    half = chip_sum.shape[0]
    peers = lax.axis_size(PLANE)
    pieces = lax.all_to_all(chip_sum.reshape(peers, half // peers, classes), PLANE, 0, 0)
    share = jnp.sum(pieces, axis=0)
    share, col_parts = lax.optimization_barrier((share, col_parts))
    share_rows = share.shape[0]

    def with_cols(k):
        part = lax.dynamic_slice_in_dim(col_parts, ((blk + k) % group) * extra, extra)
        return jnp.concatenate([share, part], axis=0)

    joined = with_cols(0)
    for part in [shift(with_cols(k), "blk", k) for k in range(1, group)]:
        joined = joined + part
    share = joined[:share_rows]
    share = share + shift(share, "zh", 1)
    degree = 0.5 * (row_total + joined[share_rows:].reshape(rows_dev, 1))
    offset = core * half + (y * lax.axis_size("x") + x) * share_rows
    local_gain = lax.dynamic_slice_in_dim(gains, offset, share_rows)
    coeffs = (local_gain[:, None] * share).astype(BF16)
    mine = to_all(coeffs, PLANE).reshape(half, classes)
    theirs = shift(mine, "core", 1)

    searches, images, dots = [], [], []
    for chunk in range(CHUNKS):
        search, rounded, dot_rz = spread(place, labels, basis, mine, theirs, tile_size, chunk)
        placed, pair = [], (rounded, rounded)
        for k in range(1, group):
            pair = both_ways(pair, k - 1)
            placed += [(-k, 0, pair[0]), (k, 0, pair[1])]
        image, dot_image = apply(
            cols, valid, place, tiles, degree, search, rounded, placed, slots, chunk
        )
        searches.append(search)
        images.append(image)
        dots.append(jnp.concatenate([dot_rz, dot_image], axis=0))
    sums = jnp.concatenate(dots, axis=1)
    sums = jnp.sum(to_all(sums, ("y", "x", "core")), axis=0)
    sums = to_all(sums, COLUMN)
    solution_out, residual_out = take_step(sums, labels, searches, images, tile_size)
    return solution_out[None], residual_out[None]


def solution(mesh):
    blk, sample = mesh.devices.shape
    fine = Mesh(mesh.devices.reshape(blk, 4, 4, 2, sample // 32), FINE)
    return jax.shard_map(
        on_device,
        mesh=fine,
        in_specs=(
            P(SAMPLE, "blk", None),
            P(SAMPLE, "blk", None),
            P(),
            P(SAMPLE, "blk", None, None, None),
            P(SAMPLE, "blk", None),
            P(SAMPLE, "blk", None),
        ),
        out_specs=(P(SAMPLE, "blk", None), P(SAMPLE, "blk", None)),
        check_vma=False,
    )
```

profile of v0, /device:TPU:1, one launch (start us, length us, event | category | flops | bytes accessed | tf_op | source)
XLA Modules:
  0.0 185.4 jit_solution(4297159153907121548)
XLA Ops:
  5.7 3.3 %collective-permute-start = (f32[512,512]{1,0:T(8,128)S(1)}, f32[512,512]{1,0:T(8,128)S(1)}, u32[]{:S(2)}, u32[]{:S(2)}) collective-permute-start(f32[512,512]{1,0:T(8,128)S(1)} %project_other.1), channel_id=1, source_target_pairs={{0,1},{1,0},{2,3},{3,2},{4,5},{5,4},{6,7},{7,6},{8,9},{9,8},{10,11... | collective-permute-start | bytes 3145736 | tf_op jit(solution)/shard_map/ppermute | solution.py:27
  9.0 2.1 %project_own.1 = f32[512,512]{1,0:T(8,128)S(1)} custom-call(s32[2]{0:T(128)S(1)} %pad_add_fusion.place, bf16[1024,1024]{1,0:T(8,128)(2,1)S(1)} %bitcast.18, bf16[1024,512]{1,0:T(8,128)(2,1)S(1)} %bitcast.25), custom_call_target="tpu_custom_call" | custom-call | flops 536870912 | bytes 2097152 | tf_op jit(solution)/shard_map/project_own/pallas_call | solution.py:71
  12.5 5.1 %all-to-all-start = ((f32[16,32,512]{2,1,0:T(8,128)}), f32[16,32,512]{2,1,0:T(8,128)}, u32[]{:S(2)}, u32[]{:S(2)}) async-start(f32[16,32,512]{2,1,0:T(8,128)} %bitcast.5), calls=%async_computation | async-start | bytes 2097152 | tf_op jit(solution)/shard_map/all_to_all | solution.py:362
  18.8 4.5 %degree_parts.1 = (f32[1024,1]{1,0:T(8,128)}, f32[16,256]{1,0:T(8,128)}) custom-call(s32[16]{0:T(128)} %reshape.27.cols, s32[16]{0:T(128)} %reshape.28.valid, bf16[16,256,256]{2,1,0:T(8,128)(2,1)} %bitcast.28), custom_call_target="tpu_custom_call" | custom-call | flops 4194304 | bytes 2097152 | tf_op jit(solution)/shard_map/degree_parts/pallas_call | solution.py:111
  24.2 9.7 %all-to-all-done = f32[16,32,512]{2,1,0:T(8,128)} async-done(((f32[16,32,512]{2,1,0:T(8,128)}), f32[16,32,512]{2,1,0:T(8,128)}, u32[]{:S(2)}, u32[]{:S(2)}) %all-to-all-start) | async-done | bytes 1048608 | tf_op jit(solution)/shard_map/all_to_all | solution.py:362
  37.0 3.0 %collective-permute-start.2 = (f32[34,512]{1,0:T(8,128)S(1)}, f32[34,512]{1,0:T(8,128)S(1)}, u32[]{:S(2)}, u32[]{:S(2)}) collective-permute-start(f32[34,512]{1,0:T(8,128)S(1)} %get-tuple-element.39), channel_id=1, source_target_pairs={{0,128},{64,192},{128,0},{192,64},{1,129},{65,193},{129,1},{193,65... | collective-permute-start | bytes 208904 | tf_op jit(solution)/shard_map/ppermute | solution.py:27
  41.6 2.3 %collective-permute-done.2 = f32[34,512]{1,0:T(8,128)S(1)} collective-permute-done((f32[34,512]{1,0:T(8,128)S(1)}, f32[34,512]{1,0:T(8,128)S(1)}, u32[]{:S(2)}, u32[]{:S(2)}) %collective-permute-start.2) | collective-permute-done | bytes 69664 | tf_op jit(solution)/shard_map/ppermute | solution.py:27
  45.4 3.7 %collective-permute-start.4 = (f32[32,512]{1,0:T(8,128)S(1)}, f32[32,512]{1,0:T(8,128)S(1)}, u32[]{:S(2)}, u32[]{:S(2)}) collective-permute-start(f32[32,512]{1,0:T(8,128)S(1)} %slice.8), channel_id=1, source_target_pairs={{0,2},{2,0},{1,3},{3,1},{4,6},{6,4},{5,7},{7,5},{8,10},{10,8},{9,1... | collective-permute-start | bytes 196616 | tf_op jit(solution)/shard_map/ppermute | solution.py:27
  49.8 2.8 %collective-permute-done.4 = f32[32,512]{1,0:T(8,128)S(1)} collective-permute-done((f32[32,512]{1,0:T(8,128)S(1)}, f32[32,512]{1,0:T(8,128)S(1)}, u32[]{:S(2)}, u32[]{:S(2)}) %collective-permute-start.4) | collective-permute-done | bytes 65568 | tf_op jit(solution)/shard_map/ppermute | solution.py:27
  52.7 14.7 %all_to_all.20 = bf16[16,32,512]{2,1,0:T(8,128)(2,1)S(1)} all-to-all(bf16[16,32,512]{2,1,0:T(8,128)(2,1)S(1)} %broadcast_in_dim.10), channel_id=1, replica_groups=mesh['blk'=4,'y'=4,'x'=4,'zh'=2,'core'=2] {'y','x'}, dimensions={0} | all-to-all | bytes 1048576 | tf_op jit(solution)/shard_map/all_to_all | solution.py:52
  67.5 3.0 %collective-permute-start.5 = (bf16[512,512]{1,0:T(8,128)(2,1)S(1)}, bf16[512,512]{1,0:T(8,128)(2,1)S(1)}, u32[]{:S(2)}, u32[]{:S(2)}) collective-permute-start(bf16[512,512]{1,0:T(8,128)(2,1)S(1)} %bitcast.31), channel_id=1, source_target_pairs={{0,1},{1,0},{2,3},{3,2},{4,5},{5,4},{6,7},{7,6},{8,9},{9,8},{10,11... | collective-permute-start | bytes 1572872 | tf_op jit(solution)/shard_map/ppermute | solution.py:27
  72.0 2.4 %spread_0.1 = (f32[1024,256]{1,0:T(8,128)S(1)}, bf16[1024,256]{1,0:T(8,128)(2,1)S(1)}, f32[1,256]{1,0:T(1,128)S(1)}) custom-call(s32[2]{0:T(128)S(1)} %pad_add_fusion.place, bf16[1024,512]{1,0:T(8,128)(2,1)S(1)} %bitcast.26, bf16[1024,1024]{1,0:T(8,128)(2,1)S(1)} %bitcast.19, bf16[1024,1024]{1,0:T(8,128)(2,1)S(1)} %bitcast.20, ...), custom_call_target="tpu_custom_call" | custom-call | flops 536870912 | bytes 4194304 | tf_op jit(solution)/shard_map/spread_0/pallas_call | solution.py:188
  76.7 6.6 %collective-permute-start.6 = (bf16[1024,256]{1,0:T(8,128)(2,1)S(1)}, bf16[1024,256]{1,0:T(8,128)(2,1)S(1)}, u32[]{:S(2)}, u32[]{:S(2)}) collective-permute-start(bf16[1024,256]{1,0:T(8,128)(2,1)S(1)} %get-tuple-element.28.own), channel_id=1, source_target_pairs={{0,64},{64,128},{128,192},{1,65},{65,129},{129,193},{2,66},{66,130... | collective-permute-start | bytes 1572872 | tf_op jit(solution)/shard_map/ppermute | solution.py:36
  83.3 2.4 %spread_1.1 = (f32[1024,256]{1,0:T(8,128)S(1)}, bf16[1024,256]{1,0:T(8,128)(2,1)S(1)}, f32[1,256]{1,0:T(1,128)S(1)}) custom-call(s32[2]{0:T(128)S(1)} %pad_add_fusion.place, bf16[1024,512]{1,0:T(8,128)(2,1)S(1)} %bitcast.27, bf16[1024,1024]{1,0:T(8,128)(2,1)S(1)} %bitcast.21, bf16[1024,1024]{1,0:T(8,128)(2,1)S(1)} %bitcast.22, ...), custom_call_target="tpu_custom_call" | custom-call | flops 536870912 | bytes 4194304 | tf_op jit(solution)/shard_map/spread_1/pallas_call | solution.py:188
  88.1 4.0 %collective-permute-start.12 = (bf16[1024,256]{1,0:T(8,128)(2,1)S(1)}, bf16[1024,256]{1,0:T(8,128)(2,1)S(1)}, u32[]{:S(2)}, u32[]{:S(2)}) collective-permute-start(bf16[1024,256]{1,0:T(8,128)(2,1)S(1)} %get-tuple-element.32.own), channel_id=1, source_target_pairs={{0,64},{64,128},{128,192},{1,65},{65,129},{129,193},{2,66},{66,130... | collective-permute-start | bytes 1572872 | tf_op jit(solution)/shard_map/ppermute | solution.py:36
  96.9 7.7 %collective-permute-done.13.rest_1_ = bf16[1024,256]{1,0:T(8,128)(2,1)S(1)} collective-permute-done((bf16[1024,256]{1,0:T(8,128)(2,1)S(1)}, bf16[1024,256]{1,0:T(8,128)(2,1)S(1)}, u32[]{:S(2)}, u32[]{:S(2)}) %collective-permute-start.13) | collective-permute-done | bytes 524320 | tf_op jit(solution)/shard_map/ppermute | solution.py:36
  108.9 6.9 %collective-permute-done.9.rest_3_ = bf16[1024,256]{1,0:T(8,128)(2,1)S(1)} collective-permute-done((bf16[1024,256]{1,0:T(8,128)(2,1)S(1)}, bf16[1024,256]{1,0:T(8,128)(2,1)S(1)}, u32[]{:S(2)}, u32[]{:S(2)}) %collective-permute-start.9) | collective-permute-done | bytes 524320 | tf_op jit(solution)/shard_map/ppermute | solution.py:36
  118.6 8.5 %collective-permute-done.15.rest_3_ = bf16[1024,256]{1,0:T(8,128)(2,1)} collective-permute-done((bf16[1024,256]{1,0:T(8,128)(2,1)S(1)}, bf16[1024,256]{1,0:T(8,128)(2,1)}, u32[]{:S(2)}, u32[]{:S(2)}) %collective-permute-start.15) | collective-permute-done | bytes 524320 | tf_op jit(solution)/shard_map/ppermute | solution.py:36
  132.2 6.2 %collective-permute-done.11.rest_5_ = bf16[1024,256]{1,0:T(8,128)(2,1)} collective-permute-done((bf16[1024,256]{1,0:T(8,128)(2,1)S(1)}, bf16[1024,256]{1,0:T(8,128)(2,1)}, u32[]{:S(2)}, u32[]{:S(2)}) %collective-permute-start.11) | collective-permute-done | bytes 524320 | tf_op jit(solution)/shard_map/ppermute | solution.py:36
  144.8 3.4 %apply_0.1 = (f32[1024,256]{1,0:T(8,128)S(1)}, f32[1,256]{1,0:T(1,128)S(1)}) custom-call(s32[16]{0:T(128)S(1)} %copy-done.27, s32[16]{0:T(128)S(1)} %copy-done.28, s32[2]{0:T(128)S(1)} %pad_add_fusion.place, bf16[16,256,256]{2,1,0:T(8,128)(2,1)S(1)} %bitcast.29, f32[1024,1]{1,0:T(8,128)S(1)} %fusion.degree, f32[1024,256]{1,0:T(8,128)S(1)} %copy-done.6, ...), custom_call_target="tpu_custom_call" | custom-call | flops 536870912 | bytes 5242880 | tf_op jit(solution)/shard_map/apply_0/pallas_call | solution.py:279
  149.6 3.4 %apply_1.1 = (f32[1024,256]{1,0:T(8,128)S(1)}, f32[1,256]{1,0:T(1,128)S(1)}) custom-call(s32[16]{0:T(128)S(1)} %copy-done.27, s32[16]{0:T(128)S(1)} %copy-done.28, s32[2]{0:T(128)S(1)} %pad_add_fusion.place, bf16[16,256,256]{2,1,0:T(8,128)(2,1)S(1)} %bitcast.30, f32[1024,1]{1,0:T(8,128)S(1)} %fusion.degree, f32[1024,256]{1,0:T(8,128)S(1)} %copy-done.8, ...), custom_call_target="tpu_custom_call" | custom-call | flops 536870912 | bytes 5242880 | tf_op jit(solution)/shard_map/apply_1/pallas_call | solution.py:279
  154.1 11.7 %all_to_all.21 = f32[32,2,512]{2,1,0:T(2,128)S(1)} all-to-all(f32[32,2,512]{2,1,0:T(2,128)S(1)} %broadcast_in_dim.11), channel_id=1, replica_groups=mesh['blk'=4,'y'=4,'x'=4,'zh'=2,'core'=2] {'y','x','core'}, dimensions={0} | all-to-all | bytes 262144 | tf_op jit(solution)/shard_map/all_to_all | solution.py:52
  165.8 14.6 %all_to_all.22.sums = f32[8,2,512]{2,1,0:T(2,128)} all-to-all(f32[8,2,512]{2,1,0:T(2,128)S(1)} %broadcast_in_dim.12), channel_id=1, replica_groups=mesh['blk'=4,'y'=4,'x'=4,'zh'=2,'core'=2] {'blk','zh'}, dimensions={0} | all-to-all | bytes 65536 | tf_op jit(solution)/shard_map/all_to_all | solution.py:52
  180.4 5.0 %take_step.1 = (f32[1024,512]{1,0:T(8,128)}, f32[1024,512]{1,0:T(8,128)}) custom-call(f32[8,2,512]{2,1,0:T(2,128)} %all_to_all.22.sums, bf16[1024,512]{1,0:T(8,128)(2,1)} %bitcast.23, f32[1024,256]{1,0:T(8,128)} %copy-done.5, f32[1024,256]{1,0:T(8,128)} %copy-done.7, f32[1024,256]{1,0:T(8,128)} %copy-done.9, f32[1024,256]{1,0:T(8,128)} %copy-done.10), custom_call_target="tpu_custom_call" | custom-call | tf_op jit(solution)/shard_map/take_step/pallas_call | solution.py:331
  (108 shorter events, 47.3 us)
Async XLA Ops:
  5.7 5.6 %collective-permute-start = (f32[512,512]{1,0:T(8,128)S(1)}, f32[512,512]{1,0:T(8,128)S(1)}, u32[]{:S(2)}, u32[]{:S(2)}) collective-permute-start(f32[512,512]{1,0:T(8,128)S(1)} %project_other.1), channel_id=1, source_target_pairs={{0,1},{1,0},{2,3},{3,2},{4,5},{5,4},{6,7},{7,6},{8,9},{9,8},{10,11... | collective-permute-start | bytes 3145736 | tf_op jit(solution)/shard_map/ppermute | solution.py:27
  12.5 21.5 %all-to-all-start = ((f32[16,32,512]{2,1,0:T(8,128)}), f32[16,32,512]{2,1,0:T(8,128)}, u32[]{:S(2)}, u32[]{:S(2)}) async-start(f32[16,32,512]{2,1,0:T(8,128)} %bitcast.5), calls=%async_computation | async-start | bytes 2097152 | tf_op jit(solution)/shard_map/all_to_all | solution.py:362
  23.3 48.7 %copy-start.1 = (bf16[1,1024,1024]{2,1,0:T(8,128)(2,1)S(1)}, bf16[1,1024,1024]{2,1,0:T(8,128)(2,1)}, u32[]{:S(2)}) copy-start(bf16[1,1024,1024]{2,1,0:T(8,128)(2,1)} %param.7) | copy-start | bytes 6291460
  23.3 48.7 %copy-start.3 = (bf16[1,1024,512]{2,1,0:T(8,128)(2,1)S(1)}, bf16[1,1024,512]{2,1,0:T(8,128)(2,1)}, u32[]{:S(2)}) copy-start(bf16[1,1024,512]{2,1,0:T(8,128)(2,1)} %param.6) | copy-start | bytes 3145732
  35.3 6.3 %collective-permute-start.1 = (f32[34,512]{1,0:T(8,128)S(1)}, f32[34,512]{1,0:T(8,128)S(1)}, u32[]{:S(2)}, u32[]{:S(2)}) collective-permute-start(f32[34,512]{1,0:T(8,128)S(1)} %get-tuple-element.38), channel_id=1, source_target_pairs={{0,64},{64,128},{128,192},{192,0},{1,65},{65,129},{129,193},{193,1... | collective-permute-start | bytes 208904 | tf_op jit(solution)/shard_map/ppermute | solution.py:27
  37.0 6.9 %collective-permute-start.2 = (f32[34,512]{1,0:T(8,128)S(1)}, f32[34,512]{1,0:T(8,128)S(1)}, u32[]{:S(2)}, u32[]{:S(2)}) collective-permute-start(f32[34,512]{1,0:T(8,128)S(1)} %get-tuple-element.39), channel_id=1, source_target_pairs={{0,128},{64,192},{128,0},{192,64},{1,129},{65,193},{129,1},{193,65... | collective-permute-start | bytes 208904 | tf_op jit(solution)/shard_map/ppermute | solution.py:27
  40.0 5.4 %collective-permute-start.3 = (f32[34,512]{1,0:T(8,128)S(1)}, f32[34,512]{1,0:T(8,128)S(1)}, u32[]{:S(2)}, u32[]{:S(2)}) collective-permute-start(f32[34,512]{1,0:T(8,128)S(1)} %get-tuple-element.40), channel_id=1, source_target_pairs={{0,192},{64,0},{128,64},{192,128},{1,193},{65,1},{129,65},{193,129... | collective-permute-start | bytes 208904 | tf_op jit(solution)/shard_map/ppermute | solution.py:27
  45.4 7.2 %collective-permute-start.4 = (f32[32,512]{1,0:T(8,128)S(1)}, f32[32,512]{1,0:T(8,128)S(1)}, u32[]{:S(2)}, u32[]{:S(2)}) collective-permute-start(f32[32,512]{1,0:T(8,128)S(1)} %slice.8), channel_id=1, source_target_pairs={{0,2},{2,0},{1,3},{3,1},{4,6},{6,4},{5,7},{7,5},{8,10},{10,8},{9,1... | collective-permute-start | bytes 196616 | tf_op jit(solution)/shard_map/ppermute | solution.py:27
  67.5 4.6 %collective-permute-start.5 = (bf16[512,512]{1,0:T(8,128)(2,1)S(1)}, bf16[512,512]{1,0:T(8,128)(2,1)S(1)}, u32[]{:S(2)}, u32[]{:S(2)}) collective-permute-start(bf16[512,512]{1,0:T(8,128)(2,1)S(1)} %bitcast.31), channel_id=1, source_target_pairs={{0,1},{1,0},{2,3},{3,2},{4,5},{5,4},{6,7},{7,6},{8,9},{9,8},{10,11... | collective-permute-start | bytes 1572872 | tf_op jit(solution)/shard_map/ppermute | solution.py:27
  75.4 17.9 %collective-permute-start.7 = (bf16[1024,256]{1,0:T(8,128)(2,1)S(1)}, bf16[1024,256]{1,0:T(8,128)(2,1)S(1)}, u32[]{:S(2)}, u32[]{:S(2)}) collective-permute-start(bf16[1024,256]{1,0:T(8,128)(2,1)S(1)} %get-tuple-element.28.own), channel_id=1, source_target_pairs={{64,0},{128,64},{192,128},{65,1},{129,65},{193,129},{66,2},{130,66... | collective-permute-start | bytes 1572872 | tf_op jit(solution)/shard_map/ppermute | solution.py:36
  76.7 18.7 %collective-permute-start.6 = (bf16[1024,256]{1,0:T(8,128)(2,1)S(1)}, bf16[1024,256]{1,0:T(8,128)(2,1)S(1)}, u32[]{:S(2)}, u32[]{:S(2)}) collective-permute-start(bf16[1024,256]{1,0:T(8,128)(2,1)S(1)} %get-tuple-element.28.own), channel_id=1, source_target_pairs={{0,64},{64,128},{128,192},{1,65},{65,129},{129,193},{2,66},{66,130... | collective-permute-start | bytes 1572872 | tf_op jit(solution)/shard_map/ppermute | solution.py:36
  86.7 51.7 %copy-start.4 = (bf16[1,4,4,256,256]{4,3,2,1,0:T(8,128)(2,1)S(1)}, bf16[1,4,4,256,256]{4,3,2,1,0:T(8,128)(2,1)}, u32[]{:S(2)}) copy-start(bf16[1,4,4,256,256]{4,3,2,1,0:T(8,128)(2,1)} %param.9) | copy-start | bytes 6291460
  86.7 51.7 %copy-start.27 = (s32[16]{0:T(128)S(1)}, s32[16]{0:T(128)}, u32[]{:S(2)}) copy-start(s32[16]{0:T(128)} %reshape.27.cols) | copy-start | bytes 196
  86.7 51.7 %copy-start.28 = (s32[16]{0:T(128)S(1)}, s32[16]{0:T(128)}, u32[]{:S(2)}) copy-start(s32[16]{0:T(128)} %reshape.28.valid) | copy-start | bytes 196
  86.7 17.8 %collective-permute-start.13 = (bf16[1024,256]{1,0:T(8,128)(2,1)S(1)}, bf16[1024,256]{1,0:T(8,128)(2,1)S(1)}, u32[]{:S(2)}, u32[]{:S(2)}) collective-permute-start(bf16[1024,256]{1,0:T(8,128)(2,1)S(1)} %get-tuple-element.32.own), channel_id=1, source_target_pairs={{64,0},{128,64},{192,128},{65,1},{129,65},{193,129},{66,2},{130,66... | collective-permute-start | bytes 1572872 | tf_op jit(solution)/shard_map/ppermute | solution.py:36
  88.1 18.5 %collective-permute-start.12 = (bf16[1024,256]{1,0:T(8,128)(2,1)S(1)}, bf16[1024,256]{1,0:T(8,128)(2,1)S(1)}, u32[]{:S(2)}, u32[]{:S(2)}) collective-permute-start(bf16[1024,256]{1,0:T(8,128)(2,1)S(1)} %get-tuple-element.32.own), channel_id=1, source_target_pairs={{0,64},{64,128},{128,192},{1,65},{65,129},{129,193},{2,66},{66,130... | collective-permute-start | bytes 1572872 | tf_op jit(solution)/shard_map/ppermute | solution.py:36
  93.3 22.5 %collective-permute-start.9 = (bf16[1024,256]{1,0:T(8,128)(2,1)S(1)}, bf16[1024,256]{1,0:T(8,128)(2,1)S(1)}, u32[]{:S(2)}, u32[]{:S(2)}) collective-permute-start(bf16[1024,256]{1,0:T(8,128)(2,1)S(1)} %collective-permute-done.7.rest_1_), channel_id=1, source_target_pairs={{64,0},{128,64},{65,1},{129,65},{66,2},{130,66},{67,3},{131,67},{6... | collective-permute-start | bytes 1572872 | tf_op jit(solution)/shard_map/ppermute | solution.py:36
  95.4 21.7 %collective-permute-start.8 = (bf16[1024,256]{1,0:T(8,128)(2,1)S(1)}, bf16[1024,256]{1,0:T(8,128)(2,1)S(1)}, u32[]{:S(2)}, u32[]{:S(2)}) collective-permute-start(bf16[1024,256]{1,0:T(8,128)(2,1)S(1)} %collective-permute-done.6.rest_0_), channel_id=1, source_target_pairs={{64,128},{128,192},{65,129},{129,193},{66,130},{130,194},{67,131},... | collective-permute-start | bytes 1572872 | tf_op jit(solution)/shard_map/ppermute | solution.py:36
  104.5 22.6 %collective-permute-start.15 = (bf16[1024,256]{1,0:T(8,128)(2,1)S(1)}, bf16[1024,256]{1,0:T(8,128)(2,1)}, u32[]{:S(2)}, u32[]{:S(2)}) collective-permute-start(bf16[1024,256]{1,0:T(8,128)(2,1)S(1)} %collective-permute-done.13.rest_1_), channel_id=1, source_target_pairs={{64,0},{128,64},{65,1},{129,65},{66,2},{130,66},{67,3},{131,67},{6... | collective-permute-start | bytes 1572872 | tf_op jit(solution)/shard_map/ppermute | solution.py:36
  106.6 21.8 %collective-permute-start.14 = (bf16[1024,256]{1,0:T(8,128)(2,1)S(1)}, bf16[1024,256]{1,0:T(8,128)(2,1)}, u32[]{:S(2)}, u32[]{:S(2)}) collective-permute-start(bf16[1024,256]{1,0:T(8,128)(2,1)S(1)} %collective-permute-done.12.rest_0_), channel_id=1, source_target_pairs={{64,128},{128,192},{65,129},{129,193},{66,130},{130,194},{67,131},... | collective-permute-start | bytes 1572872 | tf_op jit(solution)/shard_map/ppermute | solution.py:36
  115.8 22.6 %collective-permute-start.11 = (bf16[1024,256]{1,0:T(8,128)(2,1)S(1)}, bf16[1024,256]{1,0:T(8,128)(2,1)}, u32[]{:S(2)}, u32[]{:S(2)}) collective-permute-start(bf16[1024,256]{1,0:T(8,128)(2,1)S(1)} %collective-permute-done.9.rest_3_), channel_id=1, source_target_pairs={{64,0},{65,1},{66,2},{67,3},{68,4},{69,5},{70,6},{71,7},{72,8},{73... | collective-permute-start | bytes 1572872 | tf_op jit(solution)/shard_map/ppermute | solution.py:36
  117.1 21.3 %collective-permute-start.10 = (bf16[1024,256]{1,0:T(8,128)(2,1)S(1)}, bf16[1024,256]{1,0:T(8,128)(2,1)}, u32[]{:S(2)}, u32[]{:S(2)}) collective-permute-start(bf16[1024,256]{1,0:T(8,128)(2,1)S(1)} %collective-permute-done.8.rest_2_), channel_id=1, source_target_pairs={{128,192},{129,193},{130,194},{131,195},{132,196},{133,197},{134,1... | collective-permute-start | bytes 1572872 | tf_op jit(solution)/shard_map/ppermute | solution.py:36
  127.1 22.5 %collective-permute-start.17 = (bf16[1024,256]{1,0:T(8,128)(2,1)}, bf16[1024,256]{1,0:T(8,128)(2,1)}, u32[]{:S(2)}, u32[]{:S(2)}) collective-permute-start(bf16[1024,256]{1,0:T(8,128)(2,1)} %collective-permute-done.15.rest_3_), channel_id=1, source_target_pairs={{64,0},{65,1},{66,2},{67,3},{68,4},{69,5},{70,6},{71,7},{72,8},{73... | collective-permute-start | bytes 1572872 | tf_op jit(solution)/shard_map/ppermute | solution.py:36
  128.4 21.2 %collective-permute-start.16 = (bf16[1024,256]{1,0:T(8,128)(2,1)}, bf16[1024,256]{1,0:T(8,128)(2,1)}, u32[]{:S(2)}, u32[]{:S(2)}) collective-permute-start(bf16[1024,256]{1,0:T(8,128)(2,1)} %collective-permute-done.14.rest_2_), channel_id=1, source_target_pairs={{128,192},{129,193},{130,194},{131,195},{132,196},{133,197},{134,1... | collective-permute-start | bytes 1572872 | tf_op jit(solution)/shard_map/ppermute | solution.py:36
  (26 other events, 103.9 us)
where the time goes:
time: 187 us; the launch traced here: 185 us
  waiting for transfers between devices  48.8 us (26%)
  starting transfers between devices  44 us (24%)
  blocking collectives  41 us (22%)
  Pallas kernels  25.4 us (14%)
  local copies, waits for them, and re-layouts  21.1 us (11%)
  other arithmetic  4 us (2%)
    all_to_all x3, blocking collectives, to_all(): return lax.all_to_all(copies, axes, 0, 0)  41 us
    ppermute x12, waiting for transfers between devices, along_line(): return lax.ppermute(value, 'blk', pairs)  30 us
    ppermute x12, starting transfers between devices, along_line(): return lax.ppermute(value, 'blk', pairs)  23.5 us
    unnamed x65, local copies, waits for them, and re-layouts  18.2 us
    ppermute x6, starting transfers between devices, shift(): lax.ppermute(value, axis, [(i, (i + by) % size) for i in range(size)])  15.5 us
    all_to_all x1, waiting for transfers between devices, on_device(): lax.all_to_all(chip_sum.reshape(peers, half // peers, classes), PLANE, 0, 0)  9.74 us
    ppermute x6, waiting for transfers between devices, shift(): lax.ppermute(value, axis, [(i, (i + by) % size) for i in range(size)])  9.05 us
    pallas_call x2, Pallas kernels, apply(): pl.pallas_call(functools.partial(apply_kernel, places), grid_spec=pltpu.P...  6.86 us
  transfers between devices with their start and end apart: 19, of which 13 were waited for; matrix products, arithmetic and copies ran while one was open for 3% of the time, Pallas kernels for 7%

commit v1 on v0

--- a/solution.py
+++ b/solution.py
@@ -65,7 +65,7 @@
 def project(place, basis, labels, own):
     rows, classes = labels.shape
     half = basis.shape[1] // 2
-    steps = 4
+    steps = 1
     part = rows // steps
     side = (lambda i, p: (i, p[0])) if own else (lambda i, p: (i, 1 - p[0]))
     return pl.pallas_call(
@@ -148,11 +148,6 @@
 def start_at(copies, step):
     for k, copy in enumerate(copies):
         pl.when(step == k)(copy.start)
-
-
-def wait_at(copies, step):
-    for k, copy in enumerate(copies):
-        pl.when(step == k)(copy.wait)
 
 
 def spread_kernel(
@@ -222,9 +217,10 @@
 
 def apply_kernel(places, cols, valid, place, tiles, degree, search, own, *rest):
     pieces, (image, dots, panel, v_search, v_image, sems, in_sems, out_sems) = rest[:-8], rest[-8:]
-    step, steps = pl.program_id(0), pl.num_programs(0)
-    slots, size, _ = tiles.shape
+    count, size, _ = tiles.shape
     rows = own.shape[0]
+    blocks = rows // size
+    slots = count // blocks
     me = place[1]
     last = panel.shape[0] // rows - 1
 
@@ -238,36 +234,29 @@
                 target = panel.at[pl.ds(at, pieces[k].shape[0]), :]
                 act(pltpu.make_async_copy(pieces[k], target, sems.at[k]))
 
-    blocks = v_search.shape[0] // size
+    copies(lambda copy: copy.start())
     loads = moves(search, v_search, in_sems, size, blocks)
     stores = moves(v_image, image, out_sems, size, blocks)
-
-    @pl.when(step == 0)
-    def _():
-        copies(lambda copy: copy.start())
-        for copy in loads:
-            copy.start()
-        dots[...] = jnp.zeros_like(dots)
-        panel[pl.ds(pl.multiple_of(me * rows, size), rows), :] = own[...]
-        copies(lambda copy: copy.wait())
-
-    wait_at(loads, step)
-    here = pl.ds(pl.multiple_of(step * size, size), size)
-    value = v_search[here, :]
-    total = value + 0.5 * (degree[...] * value)
-    for t in range(slots):
-        at = step * slots + t
-        block = panel[pl.ds(pl.multiple_of(cols[at] * size, size), size), :]
-        product = jnp.dot(tiles[t], block, preferred_element_type=F32)
-        total = total - (0.5 * valid[at].astype(F32)) * product
-    v_image[here, :] = total
-    dots[...] += jnp.sum(value * total, axis=0, keepdims=True)
-    start_at(stores, step)
-
-    @pl.when(step == steps - 1)
-    def _():
-        for copy in stores:
-            copy.wait()
+    for copy in loads:
+        copy.start()
+    panel[pl.ds(pl.multiple_of(me * rows, size), rows), :] = own[...]
+    copies(lambda copy: copy.wait())
+    sums = jnp.zeros(dots.shape, F32)
+    for b in range(blocks):
+        loads[b].wait()
+        here = pl.ds(b * size, size)
+        value = v_search[here, :]
+        total = value + 0.5 * (degree[here, :] * value)
+        for t in range(b * slots, (b + 1) * slots):
+            block = panel[pl.ds(pl.multiple_of(cols[t] * size, size), size), :]
+            product = jnp.dot(tiles[t], block, preferred_element_type=F32)
+            total = total - (0.5 * valid[t].astype(F32)) * product
+        v_image[here, :] = total
+        stores[b].start()
+        sums = sums + jnp.sum(value * total, axis=0, keepdims=True)
+    dots[...] = sums
+    for copy in stores:
+        copy.wait()
 
 
 def apply(cols, valid, place, tiles, degree, search, own, placed, slots, chunk):
@@ -280,10 +269,10 @@
         functools.partial(apply_kernel, places),
         grid_spec=pltpu.PrefetchScalarGridSpec(
             num_scalar_prefetch=3,
-            grid=(count // slots,),
+            grid=(1,),
             in_specs=[
-                pl.BlockSpec((slots, size, size), lambda i, c, v, p: (i, 0, 0)),
-                pl.BlockSpec((size, 1), lambda i, c, v, p: (i, 0)),
+                pl.BlockSpec(tiles.shape, lambda i, c, v, p: (0, 0, 0)),
+                pl.BlockSpec((rows, 1), lambda i, c, v, p: (0, 0)),
                 in_hbm,
                 pl.BlockSpec((rows, classes), lambda i, c, v, p: (0, 0)),
             ]
@@ -382,7 +371,7 @@
 
     searches, images, dots = [], [], []
     for chunk in range(CHUNKS):
-        search, rounded, dot_rz = spread(place, labels, basis, mine, theirs, tile_size, chunk)
+        search, rounded, dot_rz = spread(place, labels, basis, mine, theirs, rows_dev // 2, chunk)
         placed, pair = [], (rounded, rounded)
         for k in range(1, group):
             pair = both_ways(pair, k - 1)
@@ -396,7 +385,7 @@
     sums = jnp.concatenate(dots, axis=1)
     sums = jnp.sum(to_all(sums, ("y", "x", "core")), axis=0)
     sums = to_all(sums, COLUMN)
-    solution_out, residual_out = take_step(sums, labels, searches, images, tile_size)
+    solution_out, residual_out = take_step(sums, labels, searches, images, rows_dev // 2)
     return solution_out[None], residual_out[None]
 
 

time: 187 us -> 184 us (0.984)
  Pallas kernels: 25.4 us -> 22 us
  transfers between devices with their start and end apart: 19 -> 19, of which waited for: 13 -> 13; matrix products, arithmetic and copies ran while one was open for 3% -> 3% of each run, Pallas kernels for 7% -> 6%
where the time goes in v1:
time: 184 us; the launch traced here: 183 us
  waiting for transfers between devices  50 us (27%)
  starting transfers between devices  44 us (24%)
  blocking collectives  41.1 us (22%)
  Pallas kernels  22 us (12%)
  local copies, waits for them, and re-layouts  21.1 us (11%)
  other arithmetic  4 us (2%)
    all_to_all x3, blocking collectives, to_all(): return lax.all_to_all(copies, axes, 0, 0)  41.1 us
    ppermute x12, waiting for transfers between devices, along_line(): return lax.ppermute(value, 'blk', pairs)  30.5 us
    ppermute x12, starting transfers between devices, along_line(): return lax.ppermute(value, 'blk', pairs)  23.5 us
    unnamed x65, local copies, waits for them, and re-layouts  18.2 us
    ppermute x6, starting transfers between devices, shift(): lax.ppermute(value, axis, [(i, (i + by) % size) for i in range(size)])  15.5 us
    ppermute x6, waiting for transfers between devices, shift(): lax.ppermute(value, axis, [(i, (i + by) % size) for i in range(size)])  9.79 us
    all_to_all x1, waiting for transfers between devices, on_device(): lax.all_to_all(chip_sum.reshape(peers, half // peers, classes), PLANE, 0, 0)  9.74 us
    pallas_call x2, Pallas kernels, apply(): pl.pallas_call(functools.partial(apply_kernel, places), grid_spec=pltpu.P...  6.9 us
  transfers between devices with their start and end apart: 19, of which 13 were waited for; matrix products, arithmetic and copies ran while one was open for 3% of the time, Pallas kernels for 6%

profile of v1, /device:TPU:1, one launch (start us, length us, event | category | flops | bytes accessed | tf_op | source)
XLA Modules:
  0.0 183.3 jit_solution(3970072087986798037)
XLA Ops:
  4.8 3.3 %collective-permute-start = (f32[512,512]{1,0:T(8,128)S(1)}, f32[512,512]{1,0:T(8,128)S(1)}, u32[]{:S(2)}, u32[]{:S(2)}) collective-permute-start(f32[512,512]{1,0:T(8,128)S(1)} %project_other.1), channel_id=1, source_target_pairs={{0,1},{1,0},{2,3},{3,2},{4,5},{5,4},{6,7},{7,6},{8,9},{9,8},{10,11... | collective-permute-start | bytes 3145736 | tf_op jit(solution)/shard_map/ppermute | solution.py:27
  11.6 5.1 %all-to-all-start = ((f32[16,32,512]{2,1,0:T(8,128)}), f32[16,32,512]{2,1,0:T(8,128)}, u32[]{:S(2)}, u32[]{:S(2)}) async-start(f32[16,32,512]{2,1,0:T(8,128)} %bitcast.5), calls=%async_computation | async-start | bytes 2097152 | tf_op jit(solution)/shard_map/all_to_all | solution.py:351
  17.9 4.5 %degree_parts.1 = (f32[1024,1]{1,0:T(8,128)}, f32[16,256]{1,0:T(8,128)}) custom-call(s32[16]{0:T(128)} %reshape.27.cols, s32[16]{0:T(128)} %reshape.28.valid, bf16[16,256,256]{2,1,0:T(8,128)(2,1)} %bitcast.28), custom_call_target="tpu_custom_call" | custom-call | flops 4194304 | bytes 2097152 | tf_op jit(solution)/shard_map/degree_parts/pallas_call | solution.py:111
  23.3 9.7 %all-to-all-done = f32[16,32,512]{2,1,0:T(8,128)} async-done(((f32[16,32,512]{2,1,0:T(8,128)}), f32[16,32,512]{2,1,0:T(8,128)}, u32[]{:S(2)}, u32[]{:S(2)}) %all-to-all-start) | async-done | bytes 1048608 | tf_op jit(solution)/shard_map/all_to_all | solution.py:351
  34.4 1.7 collective-permute-start.1
  36.1 3.0 %collective-permute-start.2 = (f32[34,512]{1,0:T(8,128)S(1)}, f32[34,512]{1,0:T(8,128)S(1)}, u32[]{:S(2)}, u32[]{:S(2)}) collective-permute-start(f32[34,512]{1,0:T(8,128)S(1)} %get-tuple-element.39), channel_id=1, source_target_pairs={{0,128},{64,192},{128,0},{192,64},{1,129},{65,193},{129,1},{193,65... | collective-permute-start | bytes 208904 | tf_op jit(solution)/shard_map/ppermute | solution.py:27
  40.7 2.3 %collective-permute-done.2 = f32[34,512]{1,0:T(8,128)S(1)} collective-permute-done((f32[34,512]{1,0:T(8,128)S(1)}, f32[34,512]{1,0:T(8,128)S(1)}, u32[]{:S(2)}, u32[]{:S(2)}) %collective-permute-start.2) | collective-permute-done | bytes 69664 | tf_op jit(solution)/shard_map/ppermute | solution.py:27
  44.5 3.7 %collective-permute-start.4 = (f32[32,512]{1,0:T(8,128)S(1)}, f32[32,512]{1,0:T(8,128)S(1)}, u32[]{:S(2)}, u32[]{:S(2)}) collective-permute-start(f32[32,512]{1,0:T(8,128)S(1)} %slice.8), channel_id=1, source_target_pairs={{0,2},{2,0},{1,3},{3,1},{4,6},{6,4},{5,7},{7,5},{8,10},{10,8},{9,1... | collective-permute-start | bytes 196616 | tf_op jit(solution)/shard_map/ppermute | solution.py:27
  49.0 2.7 %collective-permute-done.4 = f32[32,512]{1,0:T(8,128)S(1)} collective-permute-done((f32[32,512]{1,0:T(8,128)S(1)}, f32[32,512]{1,0:T(8,128)S(1)}, u32[]{:S(2)}, u32[]{:S(2)}) %collective-permute-start.4) | collective-permute-done | bytes 65568 | tf_op jit(solution)/shard_map/ppermute | solution.py:27
  51.8 14.8 %all_to_all.20 = bf16[16,32,512]{2,1,0:T(8,128)(2,1)S(1)} all-to-all(bf16[16,32,512]{2,1,0:T(8,128)(2,1)S(1)} %broadcast_in_dim.10), channel_id=1, replica_groups=mesh['blk'=4,'y'=4,'x'=4,'zh'=2,'core'=2] {'y','x'}, dimensions={0} | all-to-all | bytes 1048576 | tf_op jit(solution)/shard_map/all_to_all | solution.py:52
  66.6 3.0 %collective-permute-start.5 = (bf16[512,512]{1,0:T(8,128)(2,1)S(1)}, bf16[512,512]{1,0:T(8,128)(2,1)S(1)}, u32[]{:S(2)}, u32[]{:S(2)}) collective-permute-start(bf16[512,512]{1,0:T(8,128)(2,1)S(1)} %bitcast.31), channel_id=1, source_target_pairs={{0,1},{1,0},{2,3},{3,2},{4,5},{5,4},{6,7},{7,6},{8,9},{9,8},{10,11... | collective-permute-start | bytes 1572872 | tf_op jit(solution)/shard_map/ppermute | solution.py:27
  71.2 1.9 %spread_0.1 = (f32[1024,256]{1,0:T(8,128)S(1)}, bf16[1024,256]{1,0:T(8,128)(2,1)S(1)}, f32[1,256]{1,0:T(1,128)S(1)}) custom-call(s32[2]{0:T(128)S(1)} %pad_add_fusion.place, bf16[1024,512]{1,0:T(8,128)(2,1)S(1)} %bitcast.26, bf16[1024,1024]{1,0:T(8,128)(2,1)S(1)} %bitcast.19, bf16[1024,1024]{1,0:T(8,128)(2,1)S(1)} %bitcast.20, ...), custom_call_target="tpu_custom_call" | custom-call | flops 536870912 | bytes 4194304 | tf_op jit(solution)/shard_map/spread_0/pallas_call | solution.py:183
  75.3 6.6 %collective-permute-start.6 = (bf16[1024,256]{1,0:T(8,128)(2,1)S(1)}, bf16[1024,256]{1,0:T(8,128)(2,1)S(1)}, u32[]{:S(2)}, u32[]{:S(2)}) collective-permute-start(bf16[1024,256]{1,0:T(8,128)(2,1)S(1)} %get-tuple-element.28.own), channel_id=1, source_target_pairs={{0,64},{64,128},{128,192},{1,65},{65,129},{129,193},{2,66},{66,130... | collective-permute-start | bytes 1572872 | tf_op jit(solution)/shard_map/ppermute | solution.py:36
  81.9 1.9 %spread_1.1 = (f32[1024,256]{1,0:T(8,128)S(1)}, bf16[1024,256]{1,0:T(8,128)(2,1)S(1)}, f32[1,256]{1,0:T(1,128)S(1)}) custom-call(s32[2]{0:T(128)S(1)} %pad_add_fusion.place, bf16[1024,512]{1,0:T(8,128)(2,1)S(1)} %bitcast.27, bf16[1024,1024]{1,0:T(8,128)(2,1)S(1)} %bitcast.21, bf16[1024,1024]{1,0:T(8,128)(2,1)S(1)} %bitcast.22, ...), custom_call_target="tpu_custom_call" | custom-call | flops 536870912 | bytes 4194304 | tf_op jit(solution)/shard_map/spread_1/pallas_call | solution.py:183
  86.2 4.0 %collective-permute-start.12 = (bf16[1024,256]{1,0:T(8,128)(2,1)S(1)}, bf16[1024,256]{1,0:T(8,128)(2,1)S(1)}, u32[]{:S(2)}, u32[]{:S(2)}) collective-permute-start(bf16[1024,256]{1,0:T(8,128)(2,1)S(1)} %get-tuple-element.32.own), channel_id=1, source_target_pairs={{0,64},{64,128},{128,192},{1,65},{65,129},{129,193},{2,66},{66,130... | collective-permute-start | bytes 1572872 | tf_op jit(solution)/shard_map/ppermute | solution.py:36
  95.5 7.7 %collective-permute-done.13.rest_1_ = bf16[1024,256]{1,0:T(8,128)(2,1)S(1)} collective-permute-done((bf16[1024,256]{1,0:T(8,128)(2,1)S(1)}, bf16[1024,256]{1,0:T(8,128)(2,1)S(1)}, u32[]{:S(2)}, u32[]{:S(2)}) %collective-permute-start.13) | collective-permute-done | bytes 524320 | tf_op jit(solution)/shard_map/ppermute | solution.py:36
  107.5 6.9 %collective-permute-done.9.rest_3_ = bf16[1024,256]{1,0:T(8,128)(2,1)S(1)} collective-permute-done((bf16[1024,256]{1,0:T(8,128)(2,1)S(1)}, bf16[1024,256]{1,0:T(8,128)(2,1)S(1)}, u32[]{:S(2)}, u32[]{:S(2)}) %collective-permute-start.9) | collective-permute-done | bytes 524320 | tf_op jit(solution)/shard_map/ppermute | solution.py:36
  117.2 8.5 %collective-permute-done.15.rest_3_ = bf16[1024,256]{1,0:T(8,128)(2,1)} collective-permute-done((bf16[1024,256]{1,0:T(8,128)(2,1)S(1)}, bf16[1024,256]{1,0:T(8,128)(2,1)}, u32[]{:S(2)}, u32[]{:S(2)}) %collective-permute-start.15) | collective-permute-done | bytes 524320 | tf_op jit(solution)/shard_map/ppermute | solution.py:36
  130.8 6.2 %collective-permute-done.11.rest_5_ = bf16[1024,256]{1,0:T(8,128)(2,1)} collective-permute-done((bf16[1024,256]{1,0:T(8,128)(2,1)S(1)}, bf16[1024,256]{1,0:T(8,128)(2,1)}, u32[]{:S(2)}, u32[]{:S(2)}) %collective-permute-start.11) | collective-permute-done | bytes 524320 | tf_op jit(solution)/shard_map/ppermute | solution.py:36
  143.5 3.5 %apply_0.1 = (f32[1024,256]{1,0:T(8,128)S(1)}, f32[1,256]{1,0:T(1,128)S(1)}) custom-call(s32[16]{0:T(128)S(1)} %copy-done.27, s32[16]{0:T(128)S(1)} %copy-done.28, s32[2]{0:T(128)S(1)} %pad_add_fusion.place, bf16[16,256,256]{2,1,0:T(8,128)(2,1)S(1)} %bitcast.29, f32[1024,1]{1,0:T(8,128)S(1)} %fusion.degree, f32[1024,256]{1,0:T(8,128)S(1)} %copy-done.6, ...), custom_call_target="tpu_custom_call" | custom-call | flops 536870912 | bytes 5242880 | tf_op jit(solution)/shard_map/apply_0/pallas_call | solution.py:268
  148.2 3.5 %apply_1.1 = (f32[1024,256]{1,0:T(8,128)S(1)}, f32[1,256]{1,0:T(1,128)S(1)}) custom-call(s32[16]{0:T(128)S(1)} %copy-done.27, s32[16]{0:T(128)S(1)} %copy-done.28, s32[2]{0:T(128)S(1)} %pad_add_fusion.place, bf16[16,256,256]{2,1,0:T(8,128)(2,1)S(1)} %bitcast.30, f32[1024,1]{1,0:T(8,128)S(1)} %fusion.degree, f32[1024,256]{1,0:T(8,128)S(1)} %copy-done.8, ...), custom_call_target="tpu_custom_call" | custom-call | flops 536870912 | bytes 5242880 | tf_op jit(solution)/shard_map/apply_1/pallas_call | solution.py:268
  152.7 11.7 %all_to_all.21 = f32[32,2,512]{2,1,0:T(2,128)S(1)} all-to-all(f32[32,2,512]{2,1,0:T(2,128)S(1)} %broadcast_in_dim.11), channel_id=1, replica_groups=mesh['blk'=4,'y'=4,'x'=4,'zh'=2,'core'=2] {'y','x','core'}, dimensions={0} | all-to-all | bytes 262144 | tf_op jit(solution)/shard_map/all_to_all | solution.py:52
  164.5 14.6 %all_to_all.22.sums = f32[8,2,512]{2,1,0:T(2,128)} all-to-all(f32[8,2,512]{2,1,0:T(2,128)S(1)} %broadcast_in_dim.12), channel_id=1, replica_groups=mesh['blk'=4,'y'=4,'x'=4,'zh'=2,'core'=2] {'blk','zh'}, dimensions={0} | all-to-all | bytes 65536 | tf_op jit(solution)/shard_map/all_to_all | solution.py:52
  179.1 4.2 %take_step.1 = (f32[1024,512]{1,0:T(8,128)}, f32[1024,512]{1,0:T(8,128)}) custom-call(f32[8,2,512]{2,1,0:T(2,128)} %all_to_all.22.sums, bf16[1024,512]{1,0:T(8,128)(2,1)} %bitcast.23, f32[1024,256]{1,0:T(8,128)} %copy-done.5, f32[1024,256]{1,0:T(8,128)} %copy-done.7, f32[1024,256]{1,0:T(8,128)} %copy-done.9, f32[1024,256]{1,0:T(8,128)} %copy-done.10), custom_call_target="tpu_custom_call" | custom-call | tf_op jit(solution)/shard_map/take_step/pallas_call | solution.py:320
  (108 shorter events, 47.4 us)
Async XLA Ops:
  4.8 5.6 %collective-permute-start = (f32[512,512]{1,0:T(8,128)S(1)}, f32[512,512]{1,0:T(8,128)S(1)}, u32[]{:S(2)}, u32[]{:S(2)}) collective-permute-start(f32[512,512]{1,0:T(8,128)S(1)} %project_other.1), channel_id=1, source_target_pairs={{0,1},{1,0},{2,3},{3,2},{4,5},{5,4},{6,7},{7,6},{8,9},{9,8},{10,11... | collective-permute-start | bytes 3145736 | tf_op jit(solution)/shard_map/ppermute | solution.py:27
  11.6 21.5 %all-to-all-start = ((f32[16,32,512]{2,1,0:T(8,128)}), f32[16,32,512]{2,1,0:T(8,128)}, u32[]{:S(2)}, u32[]{:S(2)}) async-start(f32[16,32,512]{2,1,0:T(8,128)} %bitcast.5), calls=%async_computation | async-start | bytes 2097152 | tf_op jit(solution)/shard_map/all_to_all | solution.py:351
  22.5 48.7 %copy-start.1 = (bf16[1,1024,1024]{2,1,0:T(8,128)(2,1)S(1)}, bf16[1,1024,1024]{2,1,0:T(8,128)(2,1)}, u32[]{:S(2)}) copy-start(bf16[1,1024,1024]{2,1,0:T(8,128)(2,1)} %param.7) | copy-start | bytes 6291460
  22.5 48.7 %copy-start.3 = (bf16[1,1024,512]{2,1,0:T(8,128)(2,1)S(1)}, bf16[1,1024,512]{2,1,0:T(8,128)(2,1)}, u32[]{:S(2)}) copy-start(bf16[1,1024,512]{2,1,0:T(8,128)(2,1)} %param.6) | copy-start | bytes 3145732
  34.4 6.3 %collective-permute-start.1 = (f32[34,512]{1,0:T(8,128)S(1)}, f32[34,512]{1,0:T(8,128)S(1)}, u32[]{:S(2)}, u32[]{:S(2)}) collective-permute-start(f32[34,512]{1,0:T(8,128)S(1)} %get-tuple-element.38), channel_id=1, source_target_pairs={{0,64},{64,128},{128,192},{192,0},{1,65},{65,129},{129,193},{193,1... | collective-permute-start | bytes 208904 | tf_op jit(solution)/shard_map/ppermute | solution.py:27
  36.1 6.9 %collective-permute-start.2 = (f32[34,512]{1,0:T(8,128)S(1)}, f32[34,512]{1,0:T(8,128)S(1)}, u32[]{:S(2)}, u32[]{:S(2)}) collective-permute-start(f32[34,512]{1,0:T(8,128)S(1)} %get-tuple-element.39), channel_id=1, source_target_pairs={{0,128},{64,192},{128,0},{192,64},{1,129},{65,193},{129,1},{193,65... | collective-permute-start | bytes 208904 | tf_op jit(solution)/shard_map/ppermute | solution.py:27
  39.1 5.4 %collective-permute-start.3 = (f32[34,512]{1,0:T(8,128)S(1)}, f32[34,512]{1,0:T(8,128)S(1)}, u32[]{:S(2)}, u32[]{:S(2)}) collective-permute-start(f32[34,512]{1,0:T(8,128)S(1)} %get-tuple-element.40), channel_id=1, source_target_pairs={{0,192},{64,0},{128,64},{192,128},{1,193},{65,1},{129,65},{193,129... | collective-permute-start | bytes 208904 | tf_op jit(solution)/shard_map/ppermute | solution.py:27
  44.5 7.1 %collective-permute-start.4 = (f32[32,512]{1,0:T(8,128)S(1)}, f32[32,512]{1,0:T(8,128)S(1)}, u32[]{:S(2)}, u32[]{:S(2)}) collective-permute-start(f32[32,512]{1,0:T(8,128)S(1)} %slice.8), channel_id=1, source_target_pairs={{0,2},{2,0},{1,3},{3,1},{4,6},{6,4},{5,7},{7,5},{8,10},{10,8},{9,1... | collective-permute-start | bytes 196616 | tf_op jit(solution)/shard_map/ppermute | solution.py:27
  66.6 4.6 %collective-permute-start.5 = (bf16[512,512]{1,0:T(8,128)(2,1)S(1)}, bf16[512,512]{1,0:T(8,128)(2,1)S(1)}, u32[]{:S(2)}, u32[]{:S(2)}) collective-permute-start(bf16[512,512]{1,0:T(8,128)(2,1)S(1)} %bitcast.31), channel_id=1, source_target_pairs={{0,1},{1,0},{2,3},{3,2},{4,5},{5,4},{6,7},{7,6},{8,9},{9,8},{10,11... | collective-permute-start | bytes 1572872 | tf_op jit(solution)/shard_map/ppermute | solution.py:27
  74.1 17.9 %collective-permute-start.7 = (bf16[1024,256]{1,0:T(8,128)(2,1)S(1)}, bf16[1024,256]{1,0:T(8,128)(2,1)S(1)}, u32[]{:S(2)}, u32[]{:S(2)}) collective-permute-start(bf16[1024,256]{1,0:T(8,128)(2,1)S(1)} %get-tuple-element.28.own), channel_id=1, source_target_pairs={{64,0},{128,64},{192,128},{65,1},{129,65},{193,129},{66,2},{130,66... | collective-permute-start | bytes 1572872 | tf_op jit(solution)/shard_map/ppermute | solution.py:36
  75.3 18.7 %collective-permute-start.6 = (bf16[1024,256]{1,0:T(8,128)(2,1)S(1)}, bf16[1024,256]{1,0:T(8,128)(2,1)S(1)}, u32[]{:S(2)}, u32[]{:S(2)}) collective-permute-start(bf16[1024,256]{1,0:T(8,128)(2,1)S(1)} %get-tuple-element.28.own), channel_id=1, source_target_pairs={{0,64},{64,128},{128,192},{1,65},{65,129},{129,193},{2,66},{66,130... | collective-permute-start | bytes 1572872 | tf_op jit(solution)/shard_map/ppermute | solution.py:36
  84.8 52.2 %copy-start.4 = (bf16[1,4,4,256,256]{4,3,2,1,0:T(8,128)(2,1)S(1)}, bf16[1,4,4,256,256]{4,3,2,1,0:T(8,128)(2,1)}, u32[]{:S(2)}) copy-start(bf16[1,4,4,256,256]{4,3,2,1,0:T(8,128)(2,1)} %param.9) | copy-start | bytes 6291460
  84.8 52.2 %copy-start.27 = (s32[16]{0:T(128)S(1)}, s32[16]{0:T(128)}, u32[]{:S(2)}) copy-start(s32[16]{0:T(128)} %reshape.27.cols) | copy-start | bytes 196
  84.8 52.2 %copy-start.28 = (s32[16]{0:T(128)S(1)}, s32[16]{0:T(128)}, u32[]{:S(2)}) copy-start(s32[16]{0:T(128)} %reshape.28.valid) | copy-start | bytes 196
  84.8 18.4 %collective-permute-start.13 = (bf16[1024,256]{1,0:T(8,128)(2,1)S(1)}, bf16[1024,256]{1,0:T(8,128)(2,1)S(1)}, u32[]{:S(2)}, u32[]{:S(2)}) collective-permute-start(bf16[1024,256]{1,0:T(8,128)(2,1)S(1)} %get-tuple-element.32.own), channel_id=1, source_target_pairs={{64,0},{128,64},{192,128},{65,1},{129,65},{193,129},{66,2},{130,66... | collective-permute-start | bytes 1572872 | tf_op jit(solution)/shard_map/ppermute | solution.py:36
  86.2 19.1 %collective-permute-start.12 = (bf16[1024,256]{1,0:T(8,128)(2,1)S(1)}, bf16[1024,256]{1,0:T(8,128)(2,1)S(1)}, u32[]{:S(2)}, u32[]{:S(2)}) collective-permute-start(bf16[1024,256]{1,0:T(8,128)(2,1)S(1)} %get-tuple-element.32.own), channel_id=1, source_target_pairs={{0,64},{64,128},{128,192},{1,65},{65,129},{129,193},{2,66},{66,130... | collective-permute-start | bytes 1572872 | tf_op jit(solution)/shard_map/ppermute | solution.py:36
  91.9 22.5 %collective-permute-start.9 = (bf16[1024,256]{1,0:T(8,128)(2,1)S(1)}, bf16[1024,256]{1,0:T(8,128)(2,1)S(1)}, u32[]{:S(2)}, u32[]{:S(2)}) collective-permute-start(bf16[1024,256]{1,0:T(8,128)(2,1)S(1)} %collective-permute-done.7.rest_1_), channel_id=1, source_target_pairs={{64,0},{128,64},{65,1},{129,65},{66,2},{130,66},{67,3},{131,67},{6... | collective-permute-start | bytes 1572872 | tf_op jit(solution)/shard_map/ppermute | solution.py:36
  94.0 21.7 %collective-permute-start.8 = (bf16[1024,256]{1,0:T(8,128)(2,1)S(1)}, bf16[1024,256]{1,0:T(8,128)(2,1)S(1)}, u32[]{:S(2)}, u32[]{:S(2)}) collective-permute-start(bf16[1024,256]{1,0:T(8,128)(2,1)S(1)} %collective-permute-done.6.rest_0_), channel_id=1, source_target_pairs={{64,128},{128,192},{65,129},{129,193},{66,130},{130,194},{67,131},... | collective-permute-start | bytes 1572872 | tf_op jit(solution)/shard_map/ppermute | solution.py:36
  103.2 22.6 %collective-permute-start.15 = (bf16[1024,256]{1,0:T(8,128)(2,1)S(1)}, bf16[1024,256]{1,0:T(8,128)(2,1)}, u32[]{:S(2)}, u32[]{:S(2)}) collective-permute-start(bf16[1024,256]{1,0:T(8,128)(2,1)S(1)} %collective-permute-done.13.rest_1_), channel_id=1, source_target_pairs={{64,0},{128,64},{65,1},{129,65},{66,2},{130,66},{67,3},{131,67},{6... | collective-permute-start | bytes 1572872 | tf_op jit(solution)/shard_map/ppermute | solution.py:36
  105.3 21.8 %collective-permute-start.14 = (bf16[1024,256]{1,0:T(8,128)(2,1)S(1)}, bf16[1024,256]{1,0:T(8,128)(2,1)}, u32[]{:S(2)}, u32[]{:S(2)}) collective-permute-start(bf16[1024,256]{1,0:T(8,128)(2,1)S(1)} %collective-permute-done.12.rest_0_), channel_id=1, source_target_pairs={{64,128},{128,192},{65,129},{129,193},{66,130},{130,194},{67,131},... | collective-permute-start | bytes 1572872 | tf_op jit(solution)/shard_map/ppermute | solution.py:36
  114.4 22.6 %collective-permute-start.11 = (bf16[1024,256]{1,0:T(8,128)(2,1)S(1)}, bf16[1024,256]{1,0:T(8,128)(2,1)}, u32[]{:S(2)}, u32[]{:S(2)}) collective-permute-start(bf16[1024,256]{1,0:T(8,128)(2,1)S(1)} %collective-permute-done.9.rest_3_), channel_id=1, source_target_pairs={{64,0},{65,1},{66,2},{67,3},{68,4},{69,5},{70,6},{71,7},{72,8},{73... | collective-permute-start | bytes 1572872 | tf_op jit(solution)/shard_map/ppermute | solution.py:36
  115.7 21.3 %collective-permute-start.10 = (bf16[1024,256]{1,0:T(8,128)(2,1)S(1)}, bf16[1024,256]{1,0:T(8,128)(2,1)}, u32[]{:S(2)}, u32[]{:S(2)}) collective-permute-start(bf16[1024,256]{1,0:T(8,128)(2,1)S(1)} %collective-permute-done.8.rest_2_), channel_id=1, source_target_pairs={{128,192},{129,193},{130,194},{131,195},{132,196},{133,197},{134,1... | collective-permute-start | bytes 1572872 | tf_op jit(solution)/shard_map/ppermute | solution.py:36
  125.7 22.5 %collective-permute-start.17 = (bf16[1024,256]{1,0:T(8,128)(2,1)}, bf16[1024,256]{1,0:T(8,128)(2,1)}, u32[]{:S(2)}, u32[]{:S(2)}) collective-permute-start(bf16[1024,256]{1,0:T(8,128)(2,1)} %collective-permute-done.15.rest_3_), channel_id=1, source_target_pairs={{64,0},{65,1},{66,2},{67,3},{68,4},{69,5},{70,6},{71,7},{72,8},{73... | collective-permute-start | bytes 1572872 | tf_op jit(solution)/shard_map/ppermute | solution.py:36
  127.0 21.2 %collective-permute-start.16 = (bf16[1024,256]{1,0:T(8,128)(2,1)}, bf16[1024,256]{1,0:T(8,128)(2,1)}, u32[]{:S(2)}, u32[]{:S(2)}) collective-permute-start(bf16[1024,256]{1,0:T(8,128)(2,1)} %collective-permute-done.14.rest_2_), channel_id=1, source_target_pairs={{128,192},{129,193},{130,194},{131,195},{132,196},{133,197},{134,1... | collective-permute-start | bytes 1572872 | tf_op jit(solution)/shard_map/ppermute | solution.py:36
  (26 other events, 105.0 us)

commit v2 on v1

--- a/solution.py
+++ b/solution.py
@@ -13,7 +13,7 @@
 SAMPLE = ("y", "x", "zh", "core")
 PLANE = ("y", "x")
 COLUMN = ("blk", "zh")
-VMEM_SOME = 16 * 1024 * 1024
+VMEM_SOME = 32 * 1024 * 1024
 VMEM_ALL = 60 * 1024 * 1024
 CHUNKS = 2
 
@@ -371,7 +371,7 @@
 
     searches, images, dots = [], [], []
     for chunk in range(CHUNKS):
-        search, rounded, dot_rz = spread(place, labels, basis, mine, theirs, rows_dev // 2, chunk)
+        search, rounded, dot_rz = spread(place, labels, basis, mine, theirs, rows_dev, chunk)
         placed, pair = [], (rounded, rounded)
         for k in range(1, group):
             pair = both_ways(pair, k - 1)

time: 184 us -> 184 us (level)
  no operation moved by 1% of the time
where the time goes in v2:
time: 184 us; the launch traced here: 183 us
  waiting for transfers between devices  50.5 us (27%)
  starting transfers between devices  44 us (24%)
  blocking collectives  41.1 us (22%)
  local copies, waits for them, and re-layouts  21.1 us (11%)
  Pallas kernels  21.1 us (11%)
  other arithmetic  4 us (2%)
    all_to_all x3, blocking collectives, to_all(): return lax.all_to_all(copies, axes, 0, 0)  41.1 us
    ppermute x12, waiting for transfers between devices, along_line(): return lax.ppermute(value, 'blk', pairs)  31 us
    ppermute x12, starting transfers between devices, along_line(): return lax.ppermute(value, 'blk', pairs)  23.4 us
    unnamed x65, local copies, waits for them, and re-layouts  18.2 us
    ppermute x6, starting transfers between devices, shift(): lax.ppermute(value, axis, [(i, (i + by) % size) for i in range(size)])  15.5 us
    ppermute x6, waiting for transfers between devices, shift(): lax.ppermute(value, axis, [(i, (i + by) % size) for i in range(size)])  9.77 us
    all_to_all x1, waiting for transfers between devices, on_device(): lax.all_to_all(chip_sum.reshape(peers, half // peers, classes), PLANE, 0, 0)  9.74 us
    pallas_call x2, Pallas kernels, apply(): pl.pallas_call(functools.partial(apply_kernel, places), grid_spec=pltpu.P...  7.07 us
  transfers between devices with their start and end apart: 19, of which 13 were waited for; matrix products, arithmetic and copies ran while one was open for 3% of the time, Pallas kernels for 6%

profile of v2, /device:TPU:1, one launch (start us, length us, event | category | flops | bytes accessed | tf_op | source)
XLA Modules:
  0.0 183.0 jit_solution(14540659471902692968)
XLA Ops:
  0.7 1.6 copy-done
  4.8 3.3 %collective-permute-start = (f32[512,512]{1,0:T(8,128)S(1)}, f32[512,512]{1,0:T(8,128)S(1)}, u32[]{:S(2)}, u32[]{:S(2)}) collective-permute-start(f32[512,512]{1,0:T(8,128)S(1)} %project_other.1), channel_id=1, source_target_pairs={{0,1},{1,0},{2,3},{3,2},{4,5},{5,4},{6,7},{7,6},{8,9},{9,8},{10,11... | collective-permute-start | bytes 3145736 | tf_op jit(solution)/shard_map/ppermute | solution.py:27
  11.6 5.1 %all-to-all-start = ((f32[16,32,512]{2,1,0:T(8,128)}), f32[16,32,512]{2,1,0:T(8,128)}, u32[]{:S(2)}, u32[]{:S(2)}) async-start(f32[16,32,512]{2,1,0:T(8,128)} %bitcast.5), calls=%async_computation | async-start | bytes 2097152 | tf_op jit(solution)/shard_map/all_to_all | solution.py:351
  17.9 4.5 %degree_parts.1 = (f32[1024,1]{1,0:T(8,128)}, f32[16,256]{1,0:T(8,128)}) custom-call(s32[16]{0:T(128)} %reshape.27.cols, s32[16]{0:T(128)} %reshape.28.valid, bf16[16,256,256]{2,1,0:T(8,128)(2,1)} %bitcast.28), custom_call_target="tpu_custom_call" | custom-call | flops 4194304 | bytes 2097152 | tf_op jit(solution)/shard_map/degree_parts/pallas_call | solution.py:111
  23.3 9.7 %all-to-all-done = f32[16,32,512]{2,1,0:T(8,128)} async-done(((f32[16,32,512]{2,1,0:T(8,128)}), f32[16,32,512]{2,1,0:T(8,128)}, u32[]{:S(2)}, u32[]{:S(2)}) %all-to-all-start) | async-done | bytes 1048608 | tf_op jit(solution)/shard_map/all_to_all | solution.py:351
  34.4 1.7 collective-permute-start.1
  36.1 3.0 %collective-permute-start.2 = (f32[34,512]{1,0:T(8,128)S(1)}, f32[34,512]{1,0:T(8,128)S(1)}, u32[]{:S(2)}, u32[]{:S(2)}) collective-permute-start(f32[34,512]{1,0:T(8,128)S(1)} %get-tuple-element.39), channel_id=1, source_target_pairs={{0,128},{64,192},{128,0},{192,64},{1,129},{65,193},{129,1},{193,65... | collective-permute-start | bytes 208904 | tf_op jit(solution)/shard_map/ppermute | solution.py:27
  40.7 2.3 %collective-permute-done.2 = f32[34,512]{1,0:T(8,128)S(1)} collective-permute-done((f32[34,512]{1,0:T(8,128)S(1)}, f32[34,512]{1,0:T(8,128)S(1)}, u32[]{:S(2)}, u32[]{:S(2)}) %collective-permute-start.2) | collective-permute-done | bytes 69664 | tf_op jit(solution)/shard_map/ppermute | solution.py:27
  44.5 3.7 %collective-permute-start.4 = (f32[32,512]{1,0:T(8,128)S(1)}, f32[32,512]{1,0:T(8,128)S(1)}, u32[]{:S(2)}, u32[]{:S(2)}) collective-permute-start(f32[32,512]{1,0:T(8,128)S(1)} %slice.8), channel_id=1, source_target_pairs={{0,2},{2,0},{1,3},{3,1},{4,6},{6,4},{5,7},{7,5},{8,10},{10,8},{9,1... | collective-permute-start | bytes 196616 | tf_op jit(solution)/shard_map/ppermute | solution.py:27
  49.0 2.6 %collective-permute-done.4 = f32[32,512]{1,0:T(8,128)S(1)} collective-permute-done((f32[32,512]{1,0:T(8,128)S(1)}, f32[32,512]{1,0:T(8,128)S(1)}, u32[]{:S(2)}, u32[]{:S(2)}) %collective-permute-start.4) | collective-permute-done | bytes 65568 | tf_op jit(solution)/shard_map/ppermute | solution.py:27
  51.8 14.8 %all_to_all.20 = bf16[16,32,512]{2,1,0:T(8,128)(2,1)S(1)} all-to-all(bf16[16,32,512]{2,1,0:T(8,128)(2,1)S(1)} %broadcast_in_dim.10), channel_id=1, replica_groups=mesh['blk'=4,'y'=4,'x'=4,'zh'=2,'core'=2] {'y','x'}, dimensions={0} | all-to-all | bytes 1048576 | tf_op jit(solution)/shard_map/all_to_all | solution.py:52
  66.6 3.0 %collective-permute-start.5 = (bf16[512,512]{1,0:T(8,128)(2,1)S(1)}, bf16[512,512]{1,0:T(8,128)(2,1)S(1)}, u32[]{:S(2)}, u32[]{:S(2)}) collective-permute-start(bf16[512,512]{1,0:T(8,128)(2,1)S(1)} %bitcast.31), channel_id=1, source_target_pairs={{0,1},{1,0},{2,3},{3,2},{4,5},{5,4},{6,7},{7,6},{8,9},{9,8},{10,11... | collective-permute-start | bytes 1572872 | tf_op jit(solution)/shard_map/ppermute | solution.py:27
  69.6 1.5 collective-permute-done.5.theirs
  74.8 6.5 %collective-permute-start.6 = (bf16[1024,256]{1,0:T(8,128)(2,1)S(1)}, bf16[1024,256]{1,0:T(8,128)(2,1)S(1)}, u32[]{:S(2)}, u32[]{:S(2)}) collective-permute-start(bf16[1024,256]{1,0:T(8,128)(2,1)S(1)} %get-tuple-element.28.own), channel_id=1, source_target_pairs={{0,64},{64,128},{128,192},{1,65},{65,129},{129,193},{2,66},{66,130... | collective-permute-start | bytes 1572872 | tf_op jit(solution)/shard_map/ppermute | solution.py:36
  85.1 4.0 %collective-permute-start.12 = (bf16[1024,256]{1,0:T(8,128)(2,1)S(1)}, bf16[1024,256]{1,0:T(8,128)(2,1)S(1)}, u32[]{:S(2)}, u32[]{:S(2)}) collective-permute-start(bf16[1024,256]{1,0:T(8,128)(2,1)S(1)} %get-tuple-element.32.own), channel_id=1, source_target_pairs={{0,64},{64,128},{128,192},{1,65},{65,129},{129,193},{2,66},{66,130... | collective-permute-start | bytes 1572872 | tf_op jit(solution)/shard_map/ppermute | solution.py:36
  94.9 7.7 %collective-permute-done.13.rest_1_ = bf16[1024,256]{1,0:T(8,128)(2,1)S(1)} collective-permute-done((bf16[1024,256]{1,0:T(8,128)(2,1)S(1)}, bf16[1024,256]{1,0:T(8,128)(2,1)S(1)}, u32[]{:S(2)}, u32[]{:S(2)}) %collective-permute-start.13) | collective-permute-done | bytes 524320 | tf_op jit(solution)/shard_map/ppermute | solution.py:36
  107.0 6.9 %collective-permute-done.9.rest_3_ = bf16[1024,256]{1,0:T(8,128)(2,1)S(1)} collective-permute-done((bf16[1024,256]{1,0:T(8,128)(2,1)S(1)}, bf16[1024,256]{1,0:T(8,128)(2,1)S(1)}, u32[]{:S(2)}, u32[]{:S(2)}) %collective-permute-start.9) | collective-permute-done | bytes 524320 | tf_op jit(solution)/shard_map/ppermute | solution.py:36
  116.6 8.5 %collective-permute-done.15.rest_3_ = bf16[1024,256]{1,0:T(8,128)(2,1)} collective-permute-done((bf16[1024,256]{1,0:T(8,128)(2,1)S(1)}, bf16[1024,256]{1,0:T(8,128)(2,1)}, u32[]{:S(2)}, u32[]{:S(2)}) %collective-permute-start.15) | collective-permute-done | bytes 524320 | tf_op jit(solution)/shard_map/ppermute | solution.py:36
  130.2 6.2 %collective-permute-done.11.rest_5_ = bf16[1024,256]{1,0:T(8,128)(2,1)} collective-permute-done((bf16[1024,256]{1,0:T(8,128)(2,1)S(1)}, bf16[1024,256]{1,0:T(8,128)(2,1)}, u32[]{:S(2)}, u32[]{:S(2)}) %collective-permute-start.11) | collective-permute-done | bytes 524320 | tf_op jit(solution)/shard_map/ppermute | solution.py:36
  142.9 3.4 %apply_0.1 = (f32[1024,256]{1,0:T(8,128)S(1)}, f32[1,256]{1,0:T(1,128)S(1)}) custom-call(s32[16]{0:T(128)S(1)} %copy-done.27, s32[16]{0:T(128)S(1)} %copy-done.28, s32[2]{0:T(128)S(1)} %pad_add_fusion.place, bf16[16,256,256]{2,1,0:T(8,128)(2,1)S(1)} %bitcast.29, f32[1024,1]{1,0:T(8,128)S(1)} %fusion.degree, f32[1024,256]{1,0:T(8,128)S(1)} %copy-done.6, ...), custom_call_target="tpu_custom_call" | custom-call | flops 536870912 | bytes 5242880 | tf_op jit(solution)/shard_map/apply_0/pallas_call | solution.py:268
  147.7 3.6 %apply_1.1 = (f32[1024,256]{1,0:T(8,128)S(1)}, f32[1,256]{1,0:T(1,128)S(1)}) custom-call(s32[16]{0:T(128)S(1)} %copy-done.27, s32[16]{0:T(128)S(1)} %copy-done.28, s32[2]{0:T(128)S(1)} %pad_add_fusion.place, bf16[16,256,256]{2,1,0:T(8,128)(2,1)S(1)} %bitcast.30, f32[1024,1]{1,0:T(8,128)S(1)} %fusion.degree, f32[1024,256]{1,0:T(8,128)S(1)} %copy-done.8, ...), custom_call_target="tpu_custom_call" | custom-call | flops 536870912 | bytes 5242880 | tf_op jit(solution)/shard_map/apply_1/pallas_call | solution.py:268
  152.4 11.7 %all_to_all.21 = f32[32,2,512]{2,1,0:T(2,128)S(1)} all-to-all(f32[32,2,512]{2,1,0:T(2,128)S(1)} %broadcast_in_dim.11), channel_id=1, replica_groups=mesh['blk'=4,'y'=4,'x'=4,'zh'=2,'core'=2] {'y','x','core'}, dimensions={0} | all-to-all | bytes 262144 | tf_op jit(solution)/shard_map/all_to_all | solution.py:52
  164.1 14.6 %all_to_all.22.sums = f32[8,2,512]{2,1,0:T(2,128)} all-to-all(f32[8,2,512]{2,1,0:T(2,128)S(1)} %broadcast_in_dim.12), channel_id=1, replica_groups=mesh['blk'=4,'y'=4,'x'=4,'zh'=2,'core'=2] {'blk','zh'}, dimensions={0} | all-to-all | bytes 65536 | tf_op jit(solution)/shard_map/all_to_all | solution.py:52
  178.7 4.2 %take_step.1 = (f32[1024,512]{1,0:T(8,128)}, f32[1024,512]{1,0:T(8,128)}) custom-call(f32[8,2,512]{2,1,0:T(2,128)} %all_to_all.22.sums, bf16[1024,512]{1,0:T(8,128)(2,1)} %bitcast.23, f32[1024,256]{1,0:T(8,128)} %copy-done.5, f32[1024,256]{1,0:T(8,128)} %copy-done.7, f32[1024,256]{1,0:T(8,128)} %copy-done.9, f32[1024,256]{1,0:T(8,128)} %copy-done.10), custom_call_target="tpu_custom_call" | custom-call | tf_op jit(solution)/shard_map/take_step/pallas_call | solution.py:320
  (108 shorter events, 47.5 us)
Async XLA Ops:
  4.8 5.6 %collective-permute-start = (f32[512,512]{1,0:T(8,128)S(1)}, f32[512,512]{1,0:T(8,128)S(1)}, u32[]{:S(2)}, u32[]{:S(2)}) collective-permute-start(f32[512,512]{1,0:T(8,128)S(1)} %project_other.1), channel_id=1, source_target_pairs={{0,1},{1,0},{2,3},{3,2},{4,5},{5,4},{6,7},{7,6},{8,9},{9,8},{10,11... | collective-permute-start | bytes 3145736 | tf_op jit(solution)/shard_map/ppermute | solution.py:27
  11.6 21.5 %all-to-all-start = ((f32[16,32,512]{2,1,0:T(8,128)}), f32[16,32,512]{2,1,0:T(8,128)}, u32[]{:S(2)}, u32[]{:S(2)}) async-start(f32[16,32,512]{2,1,0:T(8,128)} %bitcast.5), calls=%async_computation | async-start | bytes 2097152 | tf_op jit(solution)/shard_map/all_to_all | solution.py:351
  22.5 48.7 %copy-start.1 = (bf16[1,1024,1024]{2,1,0:T(8,128)(2,1)S(1)}, bf16[1,1024,1024]{2,1,0:T(8,128)(2,1)}, u32[]{:S(2)}) copy-start(bf16[1,1024,1024]{2,1,0:T(8,128)(2,1)} %param.7) | copy-start | bytes 6291460
  22.5 48.7 %copy-start.3 = (bf16[1,1024,512]{2,1,0:T(8,128)(2,1)S(1)}, bf16[1,1024,512]{2,1,0:T(8,128)(2,1)}, u32[]{:S(2)}) copy-start(bf16[1,1024,512]{2,1,0:T(8,128)(2,1)} %param.6) | copy-start | bytes 3145732
  34.4 6.3 %collective-permute-start.1 = (f32[34,512]{1,0:T(8,128)S(1)}, f32[34,512]{1,0:T(8,128)S(1)}, u32[]{:S(2)}, u32[]{:S(2)}) collective-permute-start(f32[34,512]{1,0:T(8,128)S(1)} %get-tuple-element.38), channel_id=1, source_target_pairs={{0,64},{64,128},{128,192},{192,0},{1,65},{65,129},{129,193},{193,1... | collective-permute-start | bytes 208904 | tf_op jit(solution)/shard_map/ppermute | solution.py:27
  36.1 6.9 %collective-permute-start.2 = (f32[34,512]{1,0:T(8,128)S(1)}, f32[34,512]{1,0:T(8,128)S(1)}, u32[]{:S(2)}, u32[]{:S(2)}) collective-permute-start(f32[34,512]{1,0:T(8,128)S(1)} %get-tuple-element.39), channel_id=1, source_target_pairs={{0,128},{64,192},{128,0},{192,64},{1,129},{65,193},{129,1},{193,65... | collective-permute-start | bytes 208904 | tf_op jit(solution)/shard_map/ppermute | solution.py:27
  39.1 5.3 %collective-permute-start.3 = (f32[34,512]{1,0:T(8,128)S(1)}, f32[34,512]{1,0:T(8,128)S(1)}, u32[]{:S(2)}, u32[]{:S(2)}) collective-permute-start(f32[34,512]{1,0:T(8,128)S(1)} %get-tuple-element.40), channel_id=1, source_target_pairs={{0,192},{64,0},{128,64},{192,128},{1,193},{65,1},{129,65},{193,129... | collective-permute-start | bytes 208904 | tf_op jit(solution)/shard_map/ppermute | solution.py:27
  44.5 7.1 %collective-permute-start.4 = (f32[32,512]{1,0:T(8,128)S(1)}, f32[32,512]{1,0:T(8,128)S(1)}, u32[]{:S(2)}, u32[]{:S(2)}) collective-permute-start(f32[32,512]{1,0:T(8,128)S(1)} %slice.8), channel_id=1, source_target_pairs={{0,2},{2,0},{1,3},{3,1},{4,6},{6,4},{5,7},{7,5},{8,10},{10,8},{9,1... | collective-permute-start | bytes 196616 | tf_op jit(solution)/shard_map/ppermute | solution.py:27
  66.6 4.6 %collective-permute-start.5 = (bf16[512,512]{1,0:T(8,128)(2,1)S(1)}, bf16[512,512]{1,0:T(8,128)(2,1)S(1)}, u32[]{:S(2)}, u32[]{:S(2)}) collective-permute-start(bf16[512,512]{1,0:T(8,128)(2,1)S(1)} %bitcast.31), channel_id=1, source_target_pairs={{0,1},{1,0},{2,3},{3,2},{4,5},{5,4},{6,7},{7,6},{8,9},{9,8},{10,11... | collective-permute-start | bytes 1572872 | tf_op jit(solution)/shard_map/ppermute | solution.py:27
  73.5 17.9 %collective-permute-start.7 = (bf16[1024,256]{1,0:T(8,128)(2,1)S(1)}, bf16[1024,256]{1,0:T(8,128)(2,1)S(1)}, u32[]{:S(2)}, u32[]{:S(2)}) collective-permute-start(bf16[1024,256]{1,0:T(8,128)(2,1)S(1)} %get-tuple-element.28.own), channel_id=1, source_target_pairs={{64,0},{128,64},{192,128},{65,1},{129,65},{193,129},{66,2},{130,66... | collective-permute-start | bytes 1572872 | tf_op jit(solution)/shard_map/ppermute | solution.py:36
  74.8 18.7 %collective-permute-start.6 = (bf16[1024,256]{1,0:T(8,128)(2,1)S(1)}, bf16[1024,256]{1,0:T(8,128)(2,1)S(1)}, u32[]{:S(2)}, u32[]{:S(2)}) collective-permute-start(bf16[1024,256]{1,0:T(8,128)(2,1)S(1)} %get-tuple-element.28.own), channel_id=1, source_target_pairs={{0,64},{64,128},{128,192},{1,65},{65,129},{129,193},{2,66},{66,130... | collective-permute-start | bytes 1572872 | tf_op jit(solution)/shard_map/ppermute | solution.py:36
  83.7 52.7 %copy-start.4 = (bf16[1,4,4,256,256]{4,3,2,1,0:T(8,128)(2,1)S(1)}, bf16[1,4,4,256,256]{4,3,2,1,0:T(8,128)(2,1)}, u32[]{:S(2)}) copy-start(bf16[1,4,4,256,256]{4,3,2,1,0:T(8,128)(2,1)} %param.9) | copy-start | bytes 6291460
  83.7 52.7 %copy-start.27 = (s32[16]{0:T(128)S(1)}, s32[16]{0:T(128)}, u32[]{:S(2)}) copy-start(s32[16]{0:T(128)} %reshape.27.cols) | copy-start | bytes 196
  83.7 52.7 %copy-start.28 = (s32[16]{0:T(128)S(1)}, s32[16]{0:T(128)}, u32[]{:S(2)}) copy-start(s32[16]{0:T(128)} %reshape.28.valid) | copy-start | bytes 196
  83.7 18.9 %collective-permute-start.13 = (bf16[1024,256]{1,0:T(8,128)(2,1)S(1)}, bf16[1024,256]{1,0:T(8,128)(2,1)S(1)}, u32[]{:S(2)}, u32[]{:S(2)}) collective-permute-start(bf16[1024,256]{1,0:T(8,128)(2,1)S(1)} %get-tuple-element.32.own), channel_id=1, source_target_pairs={{64,0},{128,64},{192,128},{65,1},{129,65},{193,129},{66,2},{130,66... | collective-permute-start | bytes 1572872 | tf_op jit(solution)/shard_map/ppermute | solution.py:36
  85.1 19.6 %collective-permute-start.12 = (bf16[1024,256]{1,0:T(8,128)(2,1)S(1)}, bf16[1024,256]{1,0:T(8,128)(2,1)S(1)}, u32[]{:S(2)}, u32[]{:S(2)}) collective-permute-start(bf16[1024,256]{1,0:T(8,128)(2,1)S(1)} %get-tuple-element.32.own), channel_id=1, source_target_pairs={{0,64},{64,128},{128,192},{1,65},{65,129},{129,193},{2,66},{66,130... | collective-permute-start | bytes 1572872 | tf_op jit(solution)/shard_map/ppermute | solution.py:36
  91.4 22.5 %collective-permute-start.9 = (bf16[1024,256]{1,0:T(8,128)(2,1)S(1)}, bf16[1024,256]{1,0:T(8,128)(2,1)S(1)}, u32[]{:S(2)}, u32[]{:S(2)}) collective-permute-start(bf16[1024,256]{1,0:T(8,128)(2,1)S(1)} %collective-permute-done.7.rest_1_), channel_id=1, source_target_pairs={{64,0},{128,64},{65,1},{129,65},{66,2},{130,66},{67,3},{131,67},{6... | collective-permute-start | bytes 1572872 | tf_op jit(solution)/shard_map/ppermute | solution.py:36
  93.5 21.7 %collective-permute-start.8 = (bf16[1024,256]{1,0:T(8,128)(2,1)S(1)}, bf16[1024,256]{1,0:T(8,128)(2,1)S(1)}, u32[]{:S(2)}, u32[]{:S(2)}) collective-permute-start(bf16[1024,256]{1,0:T(8,128)(2,1)S(1)} %collective-permute-done.6.rest_0_), channel_id=1, source_target_pairs={{64,128},{128,192},{65,129},{129,193},{66,130},{130,194},{67,131},... | collective-permute-start | bytes 1572872 | tf_op jit(solution)/shard_map/ppermute | solution.py:36
  102.6 22.6 %collective-permute-start.15 = (bf16[1024,256]{1,0:T(8,128)(2,1)S(1)}, bf16[1024,256]{1,0:T(8,128)(2,1)}, u32[]{:S(2)}, u32[]{:S(2)}) collective-permute-start(bf16[1024,256]{1,0:T(8,128)(2,1)S(1)} %collective-permute-done.13.rest_1_), channel_id=1, source_target_pairs={{64,0},{128,64},{65,1},{129,65},{66,2},{130,66},{67,3},{131,67},{6... | collective-permute-start | bytes 1572872 | tf_op jit(solution)/shard_map/ppermute | solution.py:36
  104.7 21.8 %collective-permute-start.14 = (bf16[1024,256]{1,0:T(8,128)(2,1)S(1)}, bf16[1024,256]{1,0:T(8,128)(2,1)}, u32[]{:S(2)}, u32[]{:S(2)}) collective-permute-start(bf16[1024,256]{1,0:T(8,128)(2,1)S(1)} %collective-permute-done.12.rest_0_), channel_id=1, source_target_pairs={{64,128},{128,192},{65,129},{129,193},{66,130},{130,194},{67,131},... | collective-permute-start | bytes 1572872 | tf_op jit(solution)/shard_map/ppermute | solution.py:36
  113.8 22.6 %collective-permute-start.11 = (bf16[1024,256]{1,0:T(8,128)(2,1)S(1)}, bf16[1024,256]{1,0:T(8,128)(2,1)}, u32[]{:S(2)}, u32[]{:S(2)}) collective-permute-start(bf16[1024,256]{1,0:T(8,128)(2,1)S(1)} %collective-permute-done.9.rest_3_), channel_id=1, source_target_pairs={{64,0},{65,1},{66,2},{67,3},{68,4},{69,5},{70,6},{71,7},{72,8},{73... | collective-permute-start | bytes 1572872 | tf_op jit(solution)/shard_map/ppermute | solution.py:36
  115.2 21.3 %collective-permute-start.10 = (bf16[1024,256]{1,0:T(8,128)(2,1)S(1)}, bf16[1024,256]{1,0:T(8,128)(2,1)}, u32[]{:S(2)}, u32[]{:S(2)}) collective-permute-start(bf16[1024,256]{1,0:T(8,128)(2,1)S(1)} %collective-permute-done.8.rest_2_), channel_id=1, source_target_pairs={{128,192},{129,193},{130,194},{131,195},{132,196},{133,197},{134,1... | collective-permute-start | bytes 1572872 | tf_op jit(solution)/shard_map/ppermute | solution.py:36
  125.2 22.5 %collective-permute-start.17 = (bf16[1024,256]{1,0:T(8,128)(2,1)}, bf16[1024,256]{1,0:T(8,128)(2,1)}, u32[]{:S(2)}, u32[]{:S(2)}) collective-permute-start(bf16[1024,256]{1,0:T(8,128)(2,1)} %collective-permute-done.15.rest_3_), channel_id=1, source_target_pairs={{64,0},{65,1},{66,2},{67,3},{68,4},{69,5},{70,6},{71,7},{72,8},{73... | collective-permute-start | bytes 1572872 | tf_op jit(solution)/shard_map/ppermute | solution.py:36
  126.5 21.2 %collective-permute-start.16 = (bf16[1024,256]{1,0:T(8,128)(2,1)}, bf16[1024,256]{1,0:T(8,128)(2,1)}, u32[]{:S(2)}, u32[]{:S(2)}) collective-permute-start(bf16[1024,256]{1,0:T(8,128)(2,1)} %collective-permute-done.14.rest_2_), channel_id=1, source_target_pairs={{128,192},{129,193},{130,194},{131,195},{132,196},{133,197},{134,1... | collective-permute-start | bytes 1572872 | tf_op jit(solution)/shard_map/ppermute | solution.py:36
  (26 other events, 104.5 us)

commit v3 on v2

--- a/solution.py
+++ b/solution.py
@@ -62,12 +62,12 @@
     )
 
 
-def project(place, basis, labels, own):
+def project(place, basis, labels, own, pieces, piece):
     rows, classes = labels.shape
-    half = basis.shape[1] // 2
+    half = basis.shape[1] // (2 * pieces)
     steps = 1
     part = rows // steps
-    side = (lambda i, p: (i, p[0])) if own else (lambda i, p: (i, 1 - p[0]))
+    side = lambda i, p: (i, (p[0] if own else 1 - p[0]) * pieces + piece)
     return pl.pallas_call(
         project_kernel,
         grid_spec=pltpu.PrefetchScalarGridSpec(
@@ -84,7 +84,7 @@
         cost_estimate=pl.CostEstimate(
             flops=2 * rows * half * classes, bytes_accessed=4 * rows * half, transcendentals=0
         ),
-        name="project_own" if own else "project_other",
+        name="project_own" if own else f"project_other_{piece}",
     )(place, basis, labels)
 
 
@@ -340,8 +340,8 @@
     cols = tile_cols.reshape(-1)
     valid = tile_valid.reshape(-1)
 
-    sent = shift(project(place, basis, labels, False), "core", 1)
-    chip_sum = project(place, basis, labels, True) + sent
+    sent = [shift(project(place, basis, labels, False, 2, k), "core", 1) for k in range(2)]
+    chip_sum = project(place, basis, labels, True, 1, 0) + jnp.concatenate(sent, axis=0)
     chip_sum, later_tiles = lax.optimization_barrier((chip_sum, tiles))
     row_total, col_parts = degree_parts(later_tiles, cols, valid, row_blocks * group, slots)
     extra = rows_dev // classes

time: 184 us -> 185 us (level)
    ppermute x6 -> x7, waiting for transfers between devices: 9.77 us -> 9.6 us  [shift(): lax.ppermute(value, axis, [(i, (i + by) % size) for i in range(size)])]
    ppermute x6 -> x7, starting transfers between devices: 15.5 us -> 15.7 us  [shift(): lax.ppermute(value, axis, [(i, (i + by) % size) for i in range(size)])]
  transfers between devices with their start and end apart: 19 -> 20, of which waited for: 13 -> 12; matrix products, arithmetic and copies ran while one was open for 3% -> 3% of each run, Pallas kernels for 6% -> 6%
where the time goes in v3:
time: 185 us; the launch traced here: 184 us
  waiting for transfers between devices  50.7 us (27%)
  starting transfers between devices  44.2 us (24%)
  blocking collectives  40.6 us (22%)
  Pallas kernels  21.9 us (12%)
  local copies, waits for them, and re-layouts  21.2 us (11%)
  other arithmetic  4 us (2%)
    all_to_all x3, blocking collectives, to_all(): return lax.all_to_all(copies, axes, 0, 0)  40.6 us
    ppermute x12, waiting for transfers between devices, along_line(): return lax.ppermute(value, 'blk', pairs)  31 us
    ppermute x12, starting transfers between devices, along_line(): return lax.ppermute(value, 'blk', pairs)  23.5 us
    unnamed x65, local copies, waits for them, and re-layouts  18.2 us
    ppermute x7, starting transfers between devices, shift(): lax.ppermute(value, axis, [(i, (i + by) % size) for i in range(size)])  15.7 us
    all_to_all x1, waiting for transfers between devices, on_device(): lax.all_to_all(chip_sum.reshape(peers, half // peers, classes), PLANE, 0, 0)  10 us
    ppermute x7, waiting for transfers between devices, shift(): lax.ppermute(value, axis, [(i, (i + by) % size) for i in range(size)])  9.6 us
    pallas_call x2, Pallas kernels, apply(): pl.pallas_call(functools.partial(apply_kernel, places), grid_spec=pltpu.P...  7.09 us
  transfers between devices with their start and end apart: 20, of which 12 were waited for; matrix products, arithmetic and copies ran while one was open for 3% of the time, Pallas kernels for 6%

profile of v3, /device:TPU:1, one launch (start us, length us, event | category | flops | bytes accessed | tf_op | source)
XLA Modules:
  0.0 183.6 jit_solution(3004826869709556878)
XLA Ops:
  0.7 1.6 copy-done
  4.5 3.3 %collective-permute-start = (f32[256,512]{1,0:T(8,128)S(1)}, f32[256,512]{1,0:T(8,128)S(1)}, u32[]{:S(2)}, u32[]{:S(2)}) collective-permute-start(f32[256,512]{1,0:T(8,128)S(1)} %project_other_0.1), channel_id=1, source_target_pairs={{0,1},{1,0},{2,3},{3,2},{4,5},{5,4},{6,7},{7,6},{8,9},{9,8},{10,11... | collective-permute-start | bytes 1572872 | tf_op jit(solution)/shard_map/ppermute | solution.py:27
  12.1 5.1 %all-to-all-start = ((f32[16,32,512]{2,1,0:T(8,128)}), f32[16,32,512]{2,1,0:T(8,128)}, u32[]{:S(2)}, u32[]{:S(2)}) async-start(f32[16,32,512]{2,1,0:T(8,128)} %bitcast.5), calls=%async_computation | async-start | bytes 2097152 | tf_op jit(solution)/shard_map/all_to_all | solution.py:351
  18.5 4.5 %degree_parts.1 = (f32[1024,1]{1,0:T(8,128)}, f32[16,256]{1,0:T(8,128)}) custom-call(s32[16]{0:T(128)} %reshape.27.cols, s32[16]{0:T(128)} %reshape.28.valid, bf16[16,256,256]{2,1,0:T(8,128)(2,1)} %bitcast.30), custom_call_target="tpu_custom_call" | custom-call | flops 4194304 | bytes 2097152 | tf_op jit(solution)/shard_map/degree_parts/pallas_call | solution.py:111
  23.9 10.0 %all-to-all-done = f32[16,32,512]{2,1,0:T(8,128)} async-done(((f32[16,32,512]{2,1,0:T(8,128)}), f32[16,32,512]{2,1,0:T(8,128)}, u32[]{:S(2)}, u32[]{:S(2)}) %all-to-all-start) | async-done | bytes 1048608 | tf_op jit(solution)/shard_map/all_to_all | solution.py:351
  35.3 1.7 collective-permute-start.2
  37.0 3.0 %collective-permute-start.3 = (f32[34,512]{1,0:T(8,128)S(1)}, f32[34,512]{1,0:T(8,128)S(1)}, u32[]{:S(2)}, u32[]{:S(2)}) collective-permute-start(f32[34,512]{1,0:T(8,128)S(1)} %get-tuple-element.39), channel_id=1, source_target_pairs={{0,128},{64,192},{128,0},{192,64},{1,129},{65,193},{129,1},{193,65... | collective-permute-start | bytes 208904 | tf_op jit(solution)/shard_map/ppermute | solution.py:27
  41.6 4.0 %collective-permute-done.3 = f32[34,512]{1,0:T(8,128)S(1)} collective-permute-done((f32[34,512]{1,0:T(8,128)S(1)}, f32[34,512]{1,0:T(8,128)S(1)}, u32[]{:S(2)}, u32[]{:S(2)}) %collective-permute-start.3) | collective-permute-done | bytes 69664 | tf_op jit(solution)/shard_map/ppermute | solution.py:27
  45.7 3.8 %collective-permute-start.5 = (f32[32,512]{1,0:T(8,128)S(1)}, f32[32,512]{1,0:T(8,128)S(1)}, u32[]{:S(2)}, u32[]{:S(2)}) collective-permute-start(f32[32,512]{1,0:T(8,128)S(1)} %slice.8), channel_id=1, source_target_pairs={{0,2},{2,0},{1,3},{3,1},{4,6},{6,4},{5,7},{7,5},{8,10},{10,8},{9,1... | collective-permute-start | bytes 196616 | tf_op jit(solution)/shard_map/ppermute | solution.py:27
  50.2 2.6 %collective-permute-done.5 = f32[32,512]{1,0:T(8,128)S(1)} collective-permute-done((f32[32,512]{1,0:T(8,128)S(1)}, f32[32,512]{1,0:T(8,128)S(1)}, u32[]{:S(2)}, u32[]{:S(2)}) %collective-permute-start.5) | collective-permute-done | bytes 65568 | tf_op jit(solution)/shard_map/ppermute | solution.py:27
  53.0 14.4 %all_to_all.20 = bf16[16,32,512]{2,1,0:T(8,128)(2,1)S(1)} all-to-all(bf16[16,32,512]{2,1,0:T(8,128)(2,1)S(1)} %broadcast_in_dim.10), channel_id=1, replica_groups=mesh['blk'=4,'y'=4,'x'=4,'zh'=2,'core'=2] {'y','x'}, dimensions={0} | all-to-all | bytes 1048576 | tf_op jit(solution)/shard_map/all_to_all | solution.py:52
  67.3 3.0 %collective-permute-start.6 = (bf16[512,512]{1,0:T(8,128)(2,1)S(1)}, bf16[512,512]{1,0:T(8,128)(2,1)S(1)}, u32[]{:S(2)}, u32[]{:S(2)}) collective-permute-start(bf16[512,512]{1,0:T(8,128)(2,1)S(1)} %bitcast.33), channel_id=1, source_target_pairs={{0,1},{1,0},{2,3},{3,2},{4,5},{5,4},{6,7},{7,6},{8,9},{9,8},{10,11... | collective-permute-start | bytes 1572872 | tf_op jit(solution)/shard_map/ppermute | solution.py:27
  70.3 1.5 collective-permute-done.6.theirs
  75.5 6.6 %collective-permute-start.7 = (bf16[1024,256]{1,0:T(8,128)(2,1)S(1)}, bf16[1024,256]{1,0:T(8,128)(2,1)S(1)}, u32[]{:S(2)}, u32[]{:S(2)}) collective-permute-start(bf16[1024,256]{1,0:T(8,128)(2,1)S(1)} %get-tuple-element.28.own), channel_id=1, source_target_pairs={{0,64},{64,128},{128,192},{1,65},{65,129},{129,193},{2,66},{66,130... | collective-permute-start | bytes 1572872 | tf_op jit(solution)/shard_map/ppermute | solution.py:36
  85.9 4.0 %collective-permute-start.13 = (bf16[1024,256]{1,0:T(8,128)(2,1)S(1)}, bf16[1024,256]{1,0:T(8,128)(2,1)S(1)}, u32[]{:S(2)}, u32[]{:S(2)}) collective-permute-start(bf16[1024,256]{1,0:T(8,128)(2,1)S(1)} %get-tuple-element.32.own), channel_id=1, source_target_pairs={{0,64},{64,128},{128,192},{1,65},{65,129},{129,193},{2,66},{66,130... | collective-permute-start | bytes 1572872 | tf_op jit(solution)/shard_map/ppermute | solution.py:36
  95.7 7.7 %collective-permute-done.14.rest_1_ = bf16[1024,256]{1,0:T(8,128)(2,1)S(1)} collective-permute-done((bf16[1024,256]{1,0:T(8,128)(2,1)S(1)}, bf16[1024,256]{1,0:T(8,128)(2,1)S(1)}, u32[]{:S(2)}, u32[]{:S(2)}) %collective-permute-start.14) | collective-permute-done | bytes 524320 | tf_op jit(solution)/shard_map/ppermute | solution.py:36
  107.7 6.9 %collective-permute-done.10.rest_3_ = bf16[1024,256]{1,0:T(8,128)(2,1)S(1)} collective-permute-done((bf16[1024,256]{1,0:T(8,128)(2,1)S(1)}, bf16[1024,256]{1,0:T(8,128)(2,1)S(1)}, u32[]{:S(2)}, u32[]{:S(2)}) %collective-permute-start.10) | collective-permute-done | bytes 524320 | tf_op jit(solution)/shard_map/ppermute | solution.py:36
  117.4 8.6 %collective-permute-done.16.rest_3_ = bf16[1024,256]{1,0:T(8,128)(2,1)} collective-permute-done((bf16[1024,256]{1,0:T(8,128)(2,1)S(1)}, bf16[1024,256]{1,0:T(8,128)(2,1)}, u32[]{:S(2)}, u32[]{:S(2)}) %collective-permute-start.16) | collective-permute-done | bytes 524320 | tf_op jit(solution)/shard_map/ppermute | solution.py:36
  131.0 6.2 %collective-permute-done.12.rest_5_ = bf16[1024,256]{1,0:T(8,128)(2,1)} collective-permute-done((bf16[1024,256]{1,0:T(8,128)(2,1)S(1)}, bf16[1024,256]{1,0:T(8,128)(2,1)}, u32[]{:S(2)}, u32[]{:S(2)}) %collective-permute-start.12) | collective-permute-done | bytes 524320 | tf_op jit(solution)/shard_map/ppermute | solution.py:36
  143.6 3.5 %apply_0.1 = (f32[1024,256]{1,0:T(8,128)S(1)}, f32[1,256]{1,0:T(1,128)S(1)}) custom-call(s32[16]{0:T(128)S(1)} %copy-done.27, s32[16]{0:T(128)S(1)} %copy-done.28, s32[2]{0:T(128)S(1)} %pad_add_fusion.place, bf16[16,256,256]{2,1,0:T(8,128)(2,1)S(1)} %bitcast.31, f32[1024,1]{1,0:T(8,128)S(1)} %fusion.degree, f32[1024,256]{1,0:T(8,128)S(1)} %copy-done.6, ...), custom_call_target="tpu_custom_call" | custom-call | flops 536870912 | bytes 5242880 | tf_op jit(solution)/shard_map/apply_0/pallas_call | solution.py:268
  148.4 3.6 %apply_1.1 = (f32[1024,256]{1,0:T(8,128)S(1)}, f32[1,256]{1,0:T(1,128)S(1)}) custom-call(s32[16]{0:T(128)S(1)} %copy-done.27, s32[16]{0:T(128)S(1)} %copy-done.28, s32[2]{0:T(128)S(1)} %pad_add_fusion.place, bf16[16,256,256]{2,1,0:T(8,128)(2,1)S(1)} %bitcast.32, f32[1024,1]{1,0:T(8,128)S(1)} %fusion.degree, f32[1024,256]{1,0:T(8,128)S(1)} %copy-done.8, ...), custom_call_target="tpu_custom_call" | custom-call | flops 536870912 | bytes 5242880 | tf_op jit(solution)/shard_map/apply_1/pallas_call | solution.py:268
  153.1 11.7 %all_to_all.21 = f32[32,2,512]{2,1,0:T(2,128)S(1)} all-to-all(f32[32,2,512]{2,1,0:T(2,128)S(1)} %broadcast_in_dim.11), channel_id=1, replica_groups=mesh['blk'=4,'y'=4,'x'=4,'zh'=2,'core'=2] {'y','x','core'}, dimensions={0} | all-to-all | bytes 262144 | tf_op jit(solution)/shard_map/all_to_all | solution.py:52
  164.8 14.6 %all_to_all.22.sums = f32[8,2,512]{2,1,0:T(2,128)} all-to-all(f32[8,2,512]{2,1,0:T(2,128)S(1)} %broadcast_in_dim.12), channel_id=1, replica_groups=mesh['blk'=4,'y'=4,'x'=4,'zh'=2,'core'=2] {'blk','zh'}, dimensions={0} | all-to-all | bytes 65536 | tf_op jit(solution)/shard_map/all_to_all | solution.py:52
  179.4 4.2 %take_step.1 = (f32[1024,512]{1,0:T(8,128)}, f32[1024,512]{1,0:T(8,128)}) custom-call(f32[8,2,512]{2,1,0:T(2,128)} %all_to_all.22.sums, bf16[1024,512]{1,0:T(8,128)(2,1)} %bitcast.24, f32[1024,256]{1,0:T(8,128)} %copy-done.5, f32[1024,256]{1,0:T(8,128)} %copy-done.7, f32[1024,256]{1,0:T(8,128)} %copy-done.9, f32[1024,256]{1,0:T(8,128)} %copy-done.10), custom_call_target="tpu_custom_call" | custom-call | tf_op jit(solution)/shard_map/take_step/pallas_call | solution.py:320
  (111 shorter events, 46.5 us)
Async XLA Ops:
  4.5 5.8 %collective-permute-start = (f32[256,512]{1,0:T(8,128)S(1)}, f32[256,512]{1,0:T(8,128)S(1)}, u32[]{:S(2)}, u32[]{:S(2)}) collective-permute-start(f32[256,512]{1,0:T(8,128)S(1)} %project_other_0.1), channel_id=1, source_target_pairs={{0,1},{1,0},{2,3},{3,2},{4,5},{5,4},{6,7},{7,6},{8,9},{9,8},{10,11... | collective-permute-start | bytes 1572872 | tf_op jit(solution)/shard_map/ppermute | solution.py:27
  8.9 2.0 %collective-permute-start.1 = (f32[256,512]{1,0:T(8,128)S(1)}, f32[256,512]{1,0:T(8,128)S(1)}, u32[]{:S(2)}, u32[]{:S(2)}) collective-permute-start(f32[256,512]{1,0:T(8,128)S(1)} %project_other_1.1), channel_id=1, source_target_pairs={{0,1},{1,0},{2,3},{3,2},{4,5},{5,4},{6,7},{7,6},{8,9},{9,8},{10,11... | collective-permute-start | bytes 1572872 | tf_op jit(solution)/shard_map/ppermute | solution.py:27
  12.1 21.9 %all-to-all-start = ((f32[16,32,512]{2,1,0:T(8,128)}), f32[16,32,512]{2,1,0:T(8,128)}, u32[]{:S(2)}, u32[]{:S(2)}) async-start(f32[16,32,512]{2,1,0:T(8,128)} %bitcast.5), calls=%async_computation | async-start | bytes 2097152 | tf_op jit(solution)/shard_map/all_to_all | solution.py:351
  23.0 48.8 %copy-start.3 = (bf16[1,1024,512]{2,1,0:T(8,128)(2,1)S(1)}, bf16[1,1024,512]{2,1,0:T(8,128)(2,1)}, u32[]{:S(2)}) copy-start(bf16[1,1024,512]{2,1,0:T(8,128)(2,1)} %param.6) | copy-start | bytes 3145732
  35.3 6.3 %collective-permute-start.2 = (f32[34,512]{1,0:T(8,128)S(1)}, f32[34,512]{1,0:T(8,128)S(1)}, u32[]{:S(2)}, u32[]{:S(2)}) collective-permute-start(f32[34,512]{1,0:T(8,128)S(1)} %get-tuple-element.38), channel_id=1, source_target_pairs={{0,64},{64,128},{128,192},{192,0},{1,65},{65,129},{129,193},{193,1... | collective-permute-start | bytes 208904 | tf_op jit(solution)/shard_map/ppermute | solution.py:27
  37.0 8.6 %collective-permute-start.3 = (f32[34,512]{1,0:T(8,128)S(1)}, f32[34,512]{1,0:T(8,128)S(1)}, u32[]{:S(2)}, u32[]{:S(2)}) collective-permute-start(f32[34,512]{1,0:T(8,128)S(1)} %get-tuple-element.39), channel_id=1, source_target_pairs={{0,128},{64,192},{128,0},{192,64},{1,129},{65,193},{129,1},{193,65... | collective-permute-start | bytes 208904 | tf_op jit(solution)/shard_map/ppermute | solution.py:27
  40.0 5.6 %collective-permute-start.4 = (f32[34,512]{1,0:T(8,128)S(1)}, f32[34,512]{1,0:T(8,128)S(1)}, u32[]{:S(2)}, u32[]{:S(2)}) collective-permute-start(f32[34,512]{1,0:T(8,128)S(1)} %get-tuple-element.40), channel_id=1, source_target_pairs={{0,192},{64,0},{128,64},{192,128},{1,193},{65,1},{129,65},{193,129... | collective-permute-start | bytes 208904 | tf_op jit(solution)/shard_map/ppermute | solution.py:27
  45.7 7.1 %collective-permute-start.5 = (f32[32,512]{1,0:T(8,128)S(1)}, f32[32,512]{1,0:T(8,128)S(1)}, u32[]{:S(2)}, u32[]{:S(2)}) collective-permute-start(f32[32,512]{1,0:T(8,128)S(1)} %slice.8), channel_id=1, source_target_pairs={{0,2},{2,0},{1,3},{3,1},{4,6},{6,4},{5,7},{7,5},{8,10},{10,8},{9,1... | collective-permute-start | bytes 196616 | tf_op jit(solution)/shard_map/ppermute | solution.py:27
  67.3 4.5 %collective-permute-start.6 = (bf16[512,512]{1,0:T(8,128)(2,1)S(1)}, bf16[512,512]{1,0:T(8,128)(2,1)S(1)}, u32[]{:S(2)}, u32[]{:S(2)}) collective-permute-start(bf16[512,512]{1,0:T(8,128)(2,1)S(1)} %bitcast.33), channel_id=1, source_target_pairs={{0,1},{1,0},{2,3},{3,2},{4,5},{5,4},{6,7},{7,6},{8,9},{9,8},{10,11... | collective-permute-start | bytes 1572872 | tf_op jit(solution)/shard_map/ppermute | solution.py:27
  74.2 17.9 %collective-permute-start.8 = (bf16[1024,256]{1,0:T(8,128)(2,1)S(1)}, bf16[1024,256]{1,0:T(8,128)(2,1)S(1)}, u32[]{:S(2)}, u32[]{:S(2)}) collective-permute-start(bf16[1024,256]{1,0:T(8,128)(2,1)S(1)} %get-tuple-element.28.own), channel_id=1, source_target_pairs={{64,0},{128,64},{192,128},{65,1},{129,65},{193,129},{66,2},{130,66... | collective-permute-start | bytes 1572872 | tf_op jit(solution)/shard_map/ppermute | solution.py:36
  75.5 18.7 %collective-permute-start.7 = (bf16[1024,256]{1,0:T(8,128)(2,1)S(1)}, bf16[1024,256]{1,0:T(8,128)(2,1)S(1)}, u32[]{:S(2)}, u32[]{:S(2)}) collective-permute-start(bf16[1024,256]{1,0:T(8,128)(2,1)S(1)} %get-tuple-element.28.own), channel_id=1, source_target_pairs={{0,64},{64,128},{128,192},{1,65},{65,129},{129,193},{2,66},{66,130... | collective-permute-start | bytes 1572872 | tf_op jit(solution)/shard_map/ppermute | solution.py:36
  84.4 52.7 %copy-start.4 = (bf16[1,4,4,256,256]{4,3,2,1,0:T(8,128)(2,1)S(1)}, bf16[1,4,4,256,256]{4,3,2,1,0:T(8,128)(2,1)}, u32[]{:S(2)}) copy-start(bf16[1,4,4,256,256]{4,3,2,1,0:T(8,128)(2,1)} %param.9) | copy-start | bytes 6291460
  84.4 52.7 %copy-start.27 = (s32[16]{0:T(128)S(1)}, s32[16]{0:T(128)}, u32[]{:S(2)}) copy-start(s32[16]{0:T(128)} %reshape.27.cols) | copy-start | bytes 196
  84.4 52.7 %copy-start.28 = (s32[16]{0:T(128)S(1)}, s32[16]{0:T(128)}, u32[]{:S(2)}) copy-start(s32[16]{0:T(128)} %reshape.28.valid) | copy-start | bytes 196
  84.4 18.9 %collective-permute-start.14 = (bf16[1024,256]{1,0:T(8,128)(2,1)S(1)}, bf16[1024,256]{1,0:T(8,128)(2,1)S(1)}, u32[]{:S(2)}, u32[]{:S(2)}) collective-permute-start(bf16[1024,256]{1,0:T(8,128)(2,1)S(1)} %get-tuple-element.32.own), channel_id=1, source_target_pairs={{64,0},{128,64},{192,128},{65,1},{129,65},{193,129},{66,2},{130,66... | collective-permute-start | bytes 1572872 | tf_op jit(solution)/shard_map/ppermute | solution.py:36
  85.9 19.6 %collective-permute-start.13 = (bf16[1024,256]{1,0:T(8,128)(2,1)S(1)}, bf16[1024,256]{1,0:T(8,128)(2,1)S(1)}, u32[]{:S(2)}, u32[]{:S(2)}) collective-permute-start(bf16[1024,256]{1,0:T(8,128)(2,1)S(1)} %get-tuple-element.32.own), channel_id=1, source_target_pairs={{0,64},{64,128},{128,192},{1,65},{65,129},{129,193},{2,66},{66,130... | collective-permute-start | bytes 1572872 | tf_op jit(solution)/shard_map/ppermute | solution.py:36
  92.1 22.5 %collective-permute-start.10 = (bf16[1024,256]{1,0:T(8,128)(2,1)S(1)}, bf16[1024,256]{1,0:T(8,128)(2,1)S(1)}, u32[]{:S(2)}, u32[]{:S(2)}) collective-permute-start(bf16[1024,256]{1,0:T(8,128)(2,1)S(1)} %collective-permute-done.8.rest_1_), channel_id=1, source_target_pairs={{64,0},{128,64},{65,1},{129,65},{66,2},{130,66},{67,3},{131,67},{6... | collective-permute-start | bytes 1572872 | tf_op jit(solution)/shard_map/ppermute | solution.py:36
  94.2 21.7 %collective-permute-start.9 = (bf16[1024,256]{1,0:T(8,128)(2,1)S(1)}, bf16[1024,256]{1,0:T(8,128)(2,1)S(1)}, u32[]{:S(2)}, u32[]{:S(2)}) collective-permute-start(bf16[1024,256]{1,0:T(8,128)(2,1)S(1)} %collective-permute-done.7.rest_0_), channel_id=1, source_target_pairs={{64,128},{128,192},{65,129},{129,193},{66,130},{130,194},{67,131},... | collective-permute-start | bytes 1572872 | tf_op jit(solution)/shard_map/ppermute | solution.py:36
  103.3 22.6 %collective-permute-start.16 = (bf16[1024,256]{1,0:T(8,128)(2,1)S(1)}, bf16[1024,256]{1,0:T(8,128)(2,1)}, u32[]{:S(2)}, u32[]{:S(2)}) collective-permute-start(bf16[1024,256]{1,0:T(8,128)(2,1)S(1)} %collective-permute-done.14.rest_1_), channel_id=1, source_target_pairs={{64,0},{128,64},{65,1},{129,65},{66,2},{130,66},{67,3},{131,67},{6... | collective-permute-start | bytes 1572872 | tf_op jit(solution)/shard_map/ppermute | solution.py:36
  105.4 21.8 %collective-permute-start.15 = (bf16[1024,256]{1,0:T(8,128)(2,1)S(1)}, bf16[1024,256]{1,0:T(8,128)(2,1)}, u32[]{:S(2)}, u32[]{:S(2)}) collective-permute-start(bf16[1024,256]{1,0:T(8,128)(2,1)S(1)} %collective-permute-done.13.rest_0_), channel_id=1, source_target_pairs={{64,128},{128,192},{65,129},{129,193},{66,130},{130,194},{67,131},... | collective-permute-start | bytes 1572872 | tf_op jit(solution)/shard_map/ppermute | solution.py:36
  114.6 22.6 %collective-permute-start.12 = (bf16[1024,256]{1,0:T(8,128)(2,1)S(1)}, bf16[1024,256]{1,0:T(8,128)(2,1)}, u32[]{:S(2)}, u32[]{:S(2)}) collective-permute-start(bf16[1024,256]{1,0:T(8,128)(2,1)S(1)} %collective-permute-done.10.rest_3_), channel_id=1, source_target_pairs={{64,0},{65,1},{66,2},{67,3},{68,4},{69,5},{70,6},{71,7},{72,8},{73... | collective-permute-start | bytes 1572872 | tf_op jit(solution)/shard_map/ppermute | solution.py:36
  115.9 21.3 %collective-permute-start.11 = (bf16[1024,256]{1,0:T(8,128)(2,1)S(1)}, bf16[1024,256]{1,0:T(8,128)(2,1)}, u32[]{:S(2)}, u32[]{:S(2)}) collective-permute-start(bf16[1024,256]{1,0:T(8,128)(2,1)S(1)} %collective-permute-done.9.rest_2_), channel_id=1, source_target_pairs={{128,192},{129,193},{130,194},{131,195},{132,196},{133,197},{134,1... | collective-permute-start | bytes 1572872 | tf_op jit(solution)/shard_map/ppermute | solution.py:36
  125.9 22.5 %collective-permute-start.18 = (bf16[1024,256]{1,0:T(8,128)(2,1)}, bf16[1024,256]{1,0:T(8,128)(2,1)}, u32[]{:S(2)}, u32[]{:S(2)}) collective-permute-start(bf16[1024,256]{1,0:T(8,128)(2,1)} %collective-permute-done.16.rest_3_), channel_id=1, source_target_pairs={{64,0},{65,1},{66,2},{67,3},{68,4},{69,5},{70,6},{71,7},{72,8},{73... | collective-permute-start | bytes 1572872 | tf_op jit(solution)/shard_map/ppermute | solution.py:36
  127.2 21.2 %collective-permute-start.17 = (bf16[1024,256]{1,0:T(8,128)(2,1)}, bf16[1024,256]{1,0:T(8,128)(2,1)}, u32[]{:S(2)}, u32[]{:S(2)}) collective-permute-start(bf16[1024,256]{1,0:T(8,128)(2,1)} %collective-permute-done.15.rest_2_), channel_id=1, source_target_pairs={{128,192},{129,193},{130,194},{131,195},{132,196},{133,197},{134,1... | collective-permute-start | bytes 1572872 | tf_op jit(solution)/shard_map/ppermute | solution.py:36
  (27 other events, 152.6 us)
